TPU v7x, 512 devices: a whole 4x8x8 slice. The times are simulated.
512 devices in a mesh: gx: 32 (over x, z), gy: 16 (over y, core).
Axes of the slice: x: 4, y: 8, z: 8, core: 2. Of those that a mesh axis runs over, the one named last changes fastest.
Arguments:
- voxels: bfloat16 [256, 128, 8, 96], P('gx', 'gy'), may hold values from -6 to 6
- occupancy: int32 [256, 128, 8], P('gx', 'gy'), may hold values 0 or 1
- conv_weight: bfloat16 [27, 96, 96], replicated, may hold values from -0.125 to 0.125
- conv_bias: float32 [96], replicated, may hold values from -3 to 3
- down_weight: bfloat16 [27, 96, 96], replicated, may hold values from -0.125 to 0.125
- down_cotangent: bfloat16 [128, 64, 4, 96], P('gx', 'gy'), may hold values from -6 to 6
Outputs:
- down: bfloat16 [128, 64, 4, 96], P('gx', 'gy')
- grad_voxels: bfloat16 [256, 128, 8, 96], P('gx', 'gy')
- grad_conv: float32 [27, 96, 96], replicated
- grad_bias: float32 [96], replicated
- grad_down: float32 [27, 96, 96], replicated
Inputs may be any that keep to these rules, and one draw needn't show every extreme that they name: `occupancy`: 0 or 1 for every voxel.
All inputs are finite; a program needn't handle non-finite values. No bound on the sum of `occupancy` on one device may be relied on, other than what follows from the above.
Results may differ from a plain program's by a relative error of at most 0.006.
Values may be sent and summed in bfloat16 or wider, within the bound.
A program may use at most 64 MiB of HBM per device.

v0:
```python
import math

import jax
import jax.numpy as jnp
from jax import lax
from jax.sharding import Mesh
from jax.sharding import PartitionSpec as P

GX = ("gx_0", "gx_1")
GY = ("gy_0", "gy_1")


TAP_OFFSETS = [
    (step_x, step_y, step_z)
    for step_x in (-1, 0, 1)
    for step_y in (-1, 0, 1)
    for step_z in (-1, 0, 1)
]
PARITY_TERMS = {0: [(0, 0)], 1: [(1, 0), (-1, 1)]}


def with_halo(value, sides, width):
    for axis, dim in sides:
        peers, length = (lax.axis_size(axis), value.shape[dim])
        up = [(i, (i + 1) % peers) for i in range(peers - 1)]
        down = [(j, i) for i, j in up]
        last = lax.slice_in_dim(value, length - width, length, axis=dim)
        leading = lax.slice_in_dim(value, 0, width, axis=dim)
        before = lax.ppermute(last, axis, up)
        after = lax.ppermute(leading, axis, down)
        value = jnp.concatenate([before, value, after], axis=dim)
    return value


def from_behind(block, axis, distance):
    devices = range(lax.axis_size(axis))
    route = [(i - distance, i) for i in devices if i - distance in devices]
    return lax.ppermute(block, axis, route)


def cut_along(value, dim, peers):
    dims = value.shape
    blocks = value.reshape(*dims[:dim], peers, dims[dim] // peers, *dims[dim + 1 :])
    return jnp.moveaxis(blocks, dim, 0)


def sent_and_summed(value, axis, dim):
    blocks = cut_along(value, dim, lax.axis_size(axis))
    arrived = lax.all_to_all(blocks, axis, split_axis=0, concat_axis=0, tiled=True)
    return arrived.sum(axis=0)


def sum_by_axis(value, axes, dim):
    far, near = axes
    blocks = cut_along(value, dim, lax.axis_size(far))
    nearer = sent_and_summed(blocks, near, dim + 1)
    arrived = lax.all_to_all(nearer, far, split_axis=0, concat_axis=0, tiled=True)
    return arrived.sum(axis=0)


def rows_for(lines, peers):
    spare = -lines.shape[0] % peers
    if not spare:
        return lines
    return jnp.concatenate([lines, jnp.zeros((spare, *lines.shape[1:]), lines.dtype)])


def from_everyone(value, axis):
    copies = jnp.broadcast_to(value, (lax.axis_size(axis), *value.shape))
    return lax.all_to_all(copies, axis, split_axis=0, concat_axis=0, tiled=True)


def joined_along(blocks, dim):
    blocks = jnp.moveaxis(blocks, 0, dim)
    dims = blocks.shape
    return blocks.reshape(*dims[:dim], dims[dim] * dims[dim + 1], *dims[dim + 2 :])


def gather_axes(value, axes, dim):
    far, near = axes
    leading = from_everyone(value, far)
    blocks = jnp.swapaxes(from_everyone(leading, near), 0, 1)
    return joined_along(blocks.reshape(-1, *value.shape), dim)


def nested_sum(value, axes):
    lines = value.reshape(-1)
    own = sum_by_axis(rows_for(lines, lax.axis_size(axes[0]) * lax.axis_size(axes[1])), axes, 0)
    whole = gather_axes(own, axes, 0)
    return whole[: len(lines)].reshape(value.shape)


def conv_same(padded, weight, size_x, size_y, size_z):
    channels = padded.shape[-1]
    running = jnp.zeros((size_x * size_y * size_z, weight.shape[2]), jnp.float32)
    for tap_index, (step_x, step_y, step_z) in enumerate(TAP_OFFSETS):
        window = padded[
            1 + step_x : 1 + step_x + size_x,
            1 + step_y : 1 + step_y + size_y,
            1 + step_z : 1 + step_z + size_z,
        ]
        running = running + jnp.dot(
            window.reshape(-1, channels), weight[tap_index], preferred_element_type=jnp.float32
        )
    return running.reshape(size_x, size_y, size_z, -1)


def weight_taps(padded, grad_out, size_x, size_y, size_z):
    channels = padded.shape[-1]
    flat_grad = grad_out.reshape(-1, grad_out.shape[-1])
    pieces = []
    for step_x, step_y, step_z in TAP_OFFSETS:
        window = padded[
            1 + step_x : 1 + step_x + size_x,
            1 + step_y : 1 + step_y + size_y,
            1 + step_z : 1 + step_z + size_z,
        ]
        pieces.append(
            jnp.dot(window.reshape(-1, channels).T, flat_grad, preferred_element_type=jnp.float32)
        )
    return jnp.stack(pieces)


def stride_window(padded, step_x, step_y, step_z, size_x, size_y, size_z):
    channels = padded.shape[-1]
    return lax.slice(
        padded,
        (1 + step_x, 1 + step_y, 1 + step_z, 0),
        (
            2 + step_x + 2 * (size_x - 1),
            2 + step_y + 2 * (size_y - 1),
            2 + step_z + 2 * (size_z - 1),
            channels,
        ),
        (2, 2, 2, 1),
    )


def stride_conv(padded, weight, size_x, size_y, size_z):
    channels = padded.shape[-1]
    running = jnp.zeros((size_x * size_y * size_z, weight.shape[2]), jnp.float32)
    for tap_index, (step_x, step_y, step_z) in enumerate(TAP_OFFSETS):
        window = stride_window(padded, step_x, step_y, step_z, size_x, size_y, size_z)
        running = running + jnp.dot(
            window.reshape(-1, channels), weight[tap_index], preferred_element_type=jnp.float32
        )
    return running.reshape(size_x, size_y, size_z, -1)


def stride_weight(padded, grad_out, size_x, size_y, size_z):
    channels = padded.shape[-1]
    flat_grad = grad_out.reshape(-1, grad_out.shape[-1])
    pieces = []
    for step_x, step_y, step_z in TAP_OFFSETS:
        window = stride_window(padded, step_x, step_y, step_z, size_x, size_y, size_z)
        pieces.append(
            jnp.dot(window.reshape(-1, channels).T, flat_grad, preferred_element_type=jnp.float32)
        )
    return jnp.stack(pieces)


def fine_from_coarse(padded, weight, size_x, size_y, size_z):
    channels = padded.shape[-1]
    flipped = jnp.swapaxes(weight, 1, 2)
    blocks = []
    for parity_x in (0, 1):
        for parity_y in (0, 1):
            for parity_z in (0, 1):
                running = jnp.zeros((size_x * size_y * size_z, weight.shape[1]), jnp.float32)
                for step_x, shift_x in PARITY_TERMS[parity_x]:
                    for step_y, shift_y in PARITY_TERMS[parity_y]:
                        for step_z, shift_z in PARITY_TERMS[parity_z]:
                            tap_index = (step_x + 1) * 9 + (step_y + 1) * 3 + (step_z + 1)
                            window = padded[
                                shift_x : shift_x + size_x,
                                shift_y : shift_y + size_y,
                                shift_z : shift_z + size_z,
                            ]
                            running = running + jnp.dot(
                                window.reshape(-1, channels),
                                flipped[tap_index],
                                preferred_element_type=jnp.float32,
                            )
                blocks.append(running.reshape(size_x, size_y, size_z, -1))
    stacked = jnp.stack(blocks).reshape(2, 2, 2, size_x, size_y, size_z, -1)
    return jnp.transpose(stacked, (3, 0, 4, 1, 5, 2, 6)).reshape(
        2 * size_x, 2 * size_y, 2 * size_z, -1
    )


def on_device(voxels, occupancy, conv_weight, conv_bias, down_weight, down_cotangent):
    tile_x, tile_y, size_z, channels = voxels.shape
    half_x, half_y, half_z = (tile_x // 2, tile_y // 2, size_z // 2)
    occupied = occupancy.astype(jnp.float32)[..., None]
    masked = (voxels.astype(jnp.float32) * occupied).astype(jnp.bfloat16)
    padded_in = with_halo(masked, ((GX, 0), (GY, 1)), 1)
    padded_in = jnp.pad(padded_in, ((0, 0), (0, 0), (1, 1), (0, 0)))
    preact = conv_same(padded_in, conv_weight, tile_x, tile_y, size_z) + conv_bias
    summed = (masked.astype(jnp.float32) + jax.nn.silu(preact) * occupied).astype(jnp.bfloat16)
    coarse_live = (
        occupancy.reshape(half_x, 2, half_y, 2, half_z, 2)
        .max(axis=(1, 3, 5))
        .astype(jnp.float32)[..., None]
    )
    edge_row = from_behind(summed[tile_x - 1 :], GX, 1)
    with_row = jnp.concatenate([edge_row, summed], 0)
    edge_col = from_behind(with_row[:, tile_y - 1 :], GY, 1)
    stride_in = jnp.pad(jnp.concatenate([edge_col, with_row], 1), ((0, 0), (0, 0), (1, 0), (0, 0)))
    down = (stride_conv(stride_in, down_weight, half_x, half_y, half_z) * coarse_live).astype(
        jnp.bfloat16
    )
    grad_coarse = (down_cotangent.astype(jnp.float32) * coarse_live).astype(jnp.bfloat16)
    grad_stride = stride_weight(stride_in, grad_coarse, half_x, half_y, half_z)
    coarse_pad = jnp.pad(grad_coarse, ((1, 1), (1, 1), (0, 1), (0, 0)))
    spread = fine_from_coarse(coarse_pad, down_weight, half_x + 1, half_y + 1, half_z)[1:, 1:]
    arrived = from_behind(spread[:1], GX, -1)
    spread = jnp.concatenate([spread[1:tile_x], spread[tile_x:] + arrived], 0)
    arrived = from_behind(spread[:, :1], GY, -1)
    grad_sum = jnp.concatenate([spread[:, 1:tile_y], spread[:, tile_y:] + arrived], 1)
    sigmoid_val = jax.nn.sigmoid(preact)
    grad_pre = (grad_sum * occupied * sigmoid_val * (1.0 + preact * (1.0 - sigmoid_val))).astype(
        jnp.bfloat16
    )
    grad_bias = jnp.sum(grad_pre.astype(jnp.float32), axis=(0, 1, 2))
    grad_conv = weight_taps(padded_in, grad_pre, tile_x, tile_y, size_z)
    grad_padded = with_halo(grad_pre, ((GX, 0), (GY, 1)), 1)
    grad_padded = jnp.pad(grad_padded, ((0, 0), (0, 0), (1, 1), (0, 0)))
    back_weight = jnp.swapaxes(conv_weight[::-1], 1, 2)
    grad_in = grad_sum + conv_same(grad_padded, back_weight, tile_x, tile_y, size_z)
    grad_voxels = (grad_in * occupied).astype(jnp.bfloat16)
    grad_conv, grad_bias, grad_stride = (
        nested_sum(grad_conv, (("gx_0", "gx_1"), ("gy_0", "gy_1"))),
        nested_sum(grad_bias, (("gx_0", "gx_1"), ("gy_0", "gy_1"))),
        nested_sum(grad_stride, (("gx_0", "gx_1"), ("gy_0", "gy_1"))),
    )
    all_cells = tile_x * lax.axis_size(GX) * tile_y * lax.axis_size(GY) * size_z
    factor = 1.0 / math.sqrt(all_cells)
    return (down, grad_voxels, grad_conv * factor, grad_bias * factor, grad_stride * factor)


def solution(mesh):
    torus = Mesh(mesh.devices.reshape(4, 8, 8, 2), ("gx_0", "gx_1", "gy_0", "gy_1"))
    placed = (P(GX, GY, None, None), P(GX, GY, None), P(), P(), P(), P(GX, GY, None, None))
    return jax.shard_map(
        on_device,
        mesh=torus,
        in_specs=placed,
        out_specs=(P(GX, GY, None, None), P(GX, GY, None, None), P(), P(), P()),
        check_vma=False,
    )
```

profile of v0, /device:TPU:1, one launch (start us, length us, event | category | flops | bytes accessed | tf_op | source)
XLA Modules:
  0.0 409.4 jit_solution(11451495707125600530)
XLA Ops:
  1.4 1.0 multiply_convert_fusion.2
  2.5 1.3 collective-permute-start.1
  3.8 5.5 %collective-permute-start = (bf16[1,8,8,96]{3,2,1,0:T(8,128)(2,1)S(1)}, bf16[1,8,8,96]{3,2,1,0:T(8,128)(2,1)S(1)}, u32[]{:S(2)}, u32[]{:S(2)}) collective-permute-start(bf16[1,8,8,96]{3,2,1,0:T(8,128)(2,1)S(1)} %get-tuple-element.97), channel_id=1, source_target_pairs={{0,16},{16,32},{32,48},{48,64},{64,80},{80,96},{96,112},{112,128},... | collective-permute-start | bytes 36872 | tf_op jit(solution)/shard_map/ppermute | solution.py:29
  10.1 1.4 copy.235
  19.5 1.3 collective-permute-start.6
  21.0 7.9 %collective-permute-start.3 = (bf16[10,1,8,96]{3,2,1,0:T(8,128)(2,1)S(1)}, bf16[10,1,8,96]{3,2,1,0:T(8,128)(2,1)S(1)}, u32[]{:S(2)}, u32[]{:S(2)}) collective-permute-start(bf16[10,1,8,96]{3,2,1,0:T(8,128)(2,1)S(1)} %get-tuple-element.90), channel_id=1, source_target_pairs={{1,0},{2,1},{3,2},{4,3},{5,4},{6,5},{7,6},{8,7},{9,8},{10,9},{11,1... | collective-permute-start | bytes 46088 | tf_op jit(solution)/shard_map/ppermute | solution.py:30
  28.9 1.9 collective-permute-start.2
  30.9 1.1 collective-permute-done.2
  33.4 2.1 collective-permute-start.7
  42.7 4.3 %collective-permute-start.4 = (bf16[1,8,8,96]{3,2,1,0:T(8,128)(2,1)S(1)}, bf16[1,8,8,96]{3,2,1,0:T(8,128)(2,1)S(1)}, u32[]{:S(2)}, u32[]{:S(2)}) collective-permute-start(bf16[1,8,8,96]{3,2,1,0:T(8,128)(2,1)S(1)} %slice.994), channel_id=1, source_target_pairs={{0,16},{16,32},{32,48},{48,64},{64,80},{80,96},{96,112},{112,128},... | collective-permute-start | bytes 36872 | tf_op jit(solution)/shard_map/ppermute | solution.py:38
  46.9 1.3 collective-permute-start.9
  48.2 4.0 collective-permute-start.8
  71.1 6.7 %all-to-all-start.4 = ((f32[16,32,1]{1,2,0:T(1,128)}), f32[16,32,1]{1,2,0:T(1,128)S(1)}, u32[]{:S(2)}, u32[]{:S(2)}) async-start(f32[16,32,1]{1,2,0:T(1,128)} %copy.263), calls=%async_computation.4 | async-start | bytes 16384 | tf_op jit(solution)/shard_map/all_to_all | solution.py:49
  80.4 4.4 %all-to-all-done.4 = f32[16,32,1]{1,2,0:T(1,128)S(1)} async-done(((f32[16,32,1]{1,2,0:T(1,128)}), f32[16,32,1]{1,2,0:T(1,128)S(1)}, u32[]{:S(2)}, u32[]{:S(2)}) %all-to-all-start.4) | async-done | bytes 2080 | tf_op jit(solution)/shard_map/all_to_all | solution.py:49
  85.6 18.1 %all-to-all-start.5 = ((f32[32,1,1]{2,1,0:T(1,128)}), f32[32,1,1]{2,1,0:T(1,128)S(1)}, u32[]{:S(2)}, u32[]{:S(2)}) async-start(f32[32,1,1]{2,1,0:T(1,128)} %copy.264), calls=%async_computation.5 | async-start | bytes 32768 | tf_op jit(solution)/shard_map/all_to_all | solution.py:57
  104.6 7.7 %all-to-all-done.5 = f32[32,1,1]{2,1,0:T(1,128)S(1)} async-done(((f32[32,1,1]{2,1,0:T(1,128)}), f32[32,1,1]{2,1,0:T(1,128)S(1)}, u32[]{:S(2)}, u32[]{:S(2)}) %all-to-all-start.5) | async-done | bytes 160 | tf_op jit(solution)/shard_map/all_to_all | solution.py:57
  112.9 1.3 broadcast_in_dim.24
  114.2 3.8 all-to-all-start.6
  118.9 7.7 %all-to-all-done.6 = f32[32,1,1]{2,1,0:T(1,128)S(1)} async-done(((f32[32,1,1]{2,1,0:T(1,128)}), f32[32,1,1]{2,1,0:T(1,128)S(1)}, u32[]{:S(2)}, u32[]{:S(2)}) %all-to-all-start.6) | async-done | bytes 160 | tf_op jit(solution)/shard_map/all_to_all | solution.py:70
  127.5 6.5 %all-to-all-start.7 = ((f32[16,32,1]{1,2,0:T(1,128)}), f32[16,32,1]{1,2,0:T(1,128)S(1)}, u32[]{:S(2)}, u32[]{:S(2)}) async-start(f32[16,32,1]{1,2,0:T(1,128)} %broadcast_in_dim.25), calls=%async_computation.7 | async-start | bytes 16384 | tf_op jit(solution)/shard_map/all_to_all | solution.py:70
  134.8 3.2 reshape_reshape_reshape.8
  138.0 1.6 copy.423
  139.6 1.4 all-to-all-done.7
  141.0 5.9 %all-to-all-start = ((f32[16,32,486]{2,1,0:T(8,128)}), f32[16,32,486]{2,1,0:T(8,128)S(1)}, u32[]{:S(2)}, u32[]{:S(2)}) async-start(f32[16,32,486]{2,1,0:T(8,128)} %bitcast.1033), calls=%async_computation | async-start | bytes 2097152 | tf_op jit(solution)/shard_map/all_to_all | solution.py:49
  147.6 3.5 collective-permute-start.5
  151.8 1.9 collective-permute-start.11
  153.7 3.6 collective-permute-start.10
  158.1 11.8 %collective-permute-done.5 = bf16[9,1,8,96]{3,2,1,0:T(8,128)(2,1)S(1)} collective-permute-done((bf16[9,1,8,96]{3,2,1,0:T(8,128)(2,1)S(1)}, bf16[9,1,8,96]{3,2,1,0:T(8,128)(2,1)S(1)}, u32[]{:S(2)}, u32[]{:S(2)}) %collective-permute-start.5) | collective-permute-done | bytes 13856 | tf_op jit(solution)/shard_map/ppermute | solution.py:38
  170.8 4.7 %slice.819 = bf16[4,4,4,96]{3,2,1,0:T(4,128)(2,1)} slice(bf16[9,9,9,96]{3,2,1,0:T(8,128)(2,1)S(1)} %fusion.69), slice={[0:7:2], [0:7:2], [2:9:2], [0:96:1]} | slice | bytes 24576 | tf_op jit(solution)/shard_map/slice | solution.py:126
  175.5 4.7 %slice.821 = bf16[4,4,4,96]{3,2,1,0:T(4,128)(2,1)} slice(bf16[9,9,9,96]{3,2,1,0:T(8,128)(2,1)S(1)} %fusion.69), slice={[0:7:2], [1:8:2], [0:7:2], [0:96:1]} | slice | bytes 24576 | tf_op jit(solution)/shard_map/slice | solution.py:126
  180.2 4.8 %slice.823 = bf16[4,4,4,96]{3,2,1,0:T(4,128)(2,1)} slice(bf16[9,9,9,96]{3,2,1,0:T(8,128)(2,1)S(1)} %fusion.69), slice={[0:7:2], [1:8:2], [1:8:2], [0:96:1]} | slice | bytes 24576 | tf_op jit(solution)/shard_map/slice | solution.py:126
  185.0 4.7 %slice.825 = bf16[4,4,4,96]{3,2,1,0:T(4,128)(2,1)} slice(bf16[9,9,9,96]{3,2,1,0:T(8,128)(2,1)S(1)} %fusion.69), slice={[0:7:2], [1:8:2], [2:9:2], [0:96:1]} | slice | bytes 24576 | tf_op jit(solution)/shard_map/slice | solution.py:126
  189.7 4.8 %slice.827 = bf16[4,4,4,96]{3,2,1,0:T(4,128)(2,1)} slice(bf16[9,9,9,96]{3,2,1,0:T(8,128)(2,1)S(1)} %fusion.69), slice={[0:7:2], [2:9:2], [0:7:2], [0:96:1]} | slice | bytes 24576 | tf_op jit(solution)/shard_map/slice | solution.py:126
  194.5 4.8 %slice.829 = bf16[4,4,4,96]{3,2,1,0:T(4,128)(2,1)} slice(bf16[9,9,9,96]{3,2,1,0:T(8,128)(2,1)S(1)} %fusion.69), slice={[0:7:2], [2:9:2], [1:8:2], [0:96:1]} | slice | bytes 24576 | tf_op jit(solution)/shard_map/slice | solution.py:126
  199.2 4.7 %slice.831 = bf16[4,4,4,96]{3,2,1,0:T(4,128)(2,1)} slice(bf16[9,9,9,96]{3,2,1,0:T(8,128)(2,1)S(1)} %fusion.69), slice={[0:7:2], [2:9:2], [2:9:2], [0:96:1]} | slice | bytes 24576 | tf_op jit(solution)/shard_map/slice | solution.py:126
  204.0 4.7 %slice.833 = bf16[4,4,4,96]{3,2,1,0:T(4,128)(2,1)} slice(bf16[9,9,9,96]{3,2,1,0:T(8,128)(2,1)S(1)} %fusion.69), slice={[1:8:2], [0:7:2], [0:7:2], [0:96:1]} | slice | bytes 24576 | tf_op jit(solution)/shard_map/slice | solution.py:126
  208.7 4.8 %slice.835 = bf16[4,4,4,96]{3,2,1,0:T(4,128)(2,1)} slice(bf16[9,9,9,96]{3,2,1,0:T(8,128)(2,1)S(1)} %fusion.69), slice={[1:8:2], [0:7:2], [1:8:2], [0:96:1]} | slice | bytes 24576 | tf_op jit(solution)/shard_map/slice | solution.py:126
  213.5 4.8 %slice.837 = bf16[4,4,4,96]{3,2,1,0:T(4,128)(2,1)} slice(bf16[9,9,9,96]{3,2,1,0:T(8,128)(2,1)S(1)} %fusion.69), slice={[1:8:2], [0:7:2], [2:9:2], [0:96:1]} | slice | bytes 24576 | tf_op jit(solution)/shard_map/slice | solution.py:126
  229.8 1.0 fusion.35
  239.6 3.2 reshape_reshape_reshape.9
  242.8 1.6 copy.422
  244.7 1.4 fusion.252
  247.2 8.6 %all-to-all-start.8 = ((f32[16,32,486]{2,1,0:T(8,128)}), f32[16,32,486]{2,1,0:T(8,128)S(1)}, u32[]{:S(2)}, u32[]{:S(2)}) async-start(f32[16,32,486]{2,1,0:T(8,128)} %bitcast.1032), calls=%async_computation.8 | async-start | bytes 2097152 | tf_op jit(solution)/shard_map/all_to_all | solution.py:49
  255.8 1.1 fusion.84
  257.7 1.1 convolution_add_fusion.22
  260.5 1.6 all_to_all.55
  262.1 21.7 %all-to-all-done.8 = f32[16,32,486]{2,1,0:T(8,128)S(1)} async-done(((f32[16,32,486]{2,1,0:T(8,128)}), f32[16,32,486]{2,1,0:T(8,128)S(1)}, u32[]{:S(2)}, u32[]{:S(2)}) %all-to-all-start.8) | async-done | bytes 995360 | tf_op jit(solution)/shard_map/all_to_all | solution.py:49
  283.7 3.9 all-to-all-start.1
  288.6 7.9 %all-to-all-done.1 = f32[32,1,486]{2,1,0:T(1,128)S(1)} async-done(((f32[32,1,486]{2,1,0:T(1,128)}), f32[32,1,486]{2,1,0:T(1,128)S(1)}, u32[]{:S(2)}, u32[]{:S(2)}) %all-to-all-start.1) | async-done | bytes 62240 | tf_op jit(solution)/shard_map/all_to_all | solution.py:57
  296.5 3.9 all-to-all-start.9
  300.6 8.6 %all-to-all-done.9 = f32[32,1,486]{2,1,0:T(1,128)S(1)} async-done(((f32[32,1,486]{2,1,0:T(1,128)}), f32[32,1,486]{2,1,0:T(1,128)S(1)}, u32[]{:S(2)}, u32[]{:S(2)}) %all-to-all-start.9) | async-done | bytes 62240 | tf_op jit(solution)/shard_map/all_to_all | solution.py:57
  309.8 3.9 all-to-all-start.2
  314.0 8.6 %all-to-all-done.2 = f32[32,1,486]{2,1,0:T(1,128)S(1)} async-done(((f32[32,1,486]{2,1,0:T(1,128)}), f32[32,1,486]{2,1,0:T(1,128)S(1)}, u32[]{:S(2)}, u32[]{:S(2)}) %all-to-all-start.2) | async-done | bytes 62240 | tf_op jit(solution)/shard_map/all_to_all | solution.py:70
  323.2 4.1 all-to-all-start.10
  327.5 8.4 %all-to-all-done.10 = f32[32,1,486]{2,1,0:T(1,128)S(1)} async-done(((f32[32,1,486]{2,1,0:T(1,128)}), f32[32,1,486]{2,1,0:T(1,128)S(1)}, u32[]{:S(2)}, u32[]{:S(2)}) %all-to-all-start.10) | async-done | bytes 62240 | tf_op jit(solution)/shard_map/all_to_all | solution.py:70
  336.0 1.1 broadcast_in_dim.23
  337.1 8.3 %all-to-all-start.3 = ((f32[16,32,486]{2,1,0:T(8,128)}), f32[16,32,486]{2,1,0:T(8,128)S(1)}, u32[]{:S(2)}, u32[]{:S(2)}) async-start(f32[16,32,486]{2,1,0:T(8,128)} %broadcast_in_dim.23), calls=%async_computation.3 | async-start | bytes 2097152 | tf_op jit(solution)/shard_map/all_to_all | solution.py:70
  347.3 26.1 %all-to-all-done.3 = f32[16,32,486]{2,1,0:T(8,128)S(1)} async-done(((f32[16,32,486]{2,1,0:T(8,128)}), f32[16,32,486]{2,1,0:T(8,128)S(1)}, u32[]{:S(2)}, u32[]{:S(2)}) %all-to-all-start.3) | async-done | bytes 995360 | tf_op jit(solution)/shard_map/all_to_all | solution.py:70
  373.4 1.1 broadcast_in_dim.27
  374.5 3.7 all-to-all-start.11
  378.6 1.1 fusion.4
  381.9 2.6 mul.120
  384.5 21.5 %all-to-all-done.11 = f32[16,32,486]{2,1,0:T(8,128)S(1)} async-done(((f32[16,32,486]{2,1,0:T(8,128)}), f32[16,32,486]{2,1,0:T(8,128)S(1)}, u32[]{:S(2)}, u32[]{:S(2)}) %all-to-all-start.11) | async-done | bytes 995360 | tf_op jit(solution)/shard_map/all_to_all | solution.py:70
  406.8 2.6 mul.126
  (368 shorter events, 78.9 us)
Async XLA Ops:
  0.6 11.4 %copy-start.38 = (bf16[4,4,4,96]{3,2,1,0:T(4,128)(2,1)S(1)}, bf16[4,4,4,96]{3,2,1,0:T(4,128)(2,1)}, u32[]{:S(2)}) copy-start(bf16[4,4,4,96]{3,2,1,0:T(4,128)(2,1)} %param.11) | copy-start | bytes 36868
  1.4 19.5 %copy-start.3 = (f32[8,8,8]{2,1,0:T(8,128)}, f32[8,8,8]{2,1,0:T(8,128)S(1)}, u32[]{:S(2)}) copy-start(f32[8,8,8]{2,1,0:T(8,128)S(1)} %convert_element_type.53) | copy-start | bytes 6148
  2.5 18.5 %collective-permute-start.1 = (bf16[1,8,8,96]{3,2,1,0:T(8,128)(2,1)S(1)}, bf16[1,8,8,96]{3,2,1,0:T(8,128)(2,1)S(1)}, u32[]{:S(2)}, u32[]{:S(2)}) collective-permute-start(bf16[1,8,8,96]{3,2,1,0:T(8,128)(2,1)S(1)} %get-tuple-element.98), channel_id=1, source_target_pairs={{16,0},{32,16},{48,32},{64,48},{80,64},{96,80},{112,96},{128,112},... | collective-permute-start | bytes 36872 | tf_op jit(solution)/shard_map/ppermute | solution.py:30
  3.8 17.2 %collective-permute-start = (bf16[1,8,8,96]{3,2,1,0:T(8,128)(2,1)S(1)}, bf16[1,8,8,96]{3,2,1,0:T(8,128)(2,1)S(1)}, u32[]{:S(2)}, u32[]{:S(2)}) collective-permute-start(bf16[1,8,8,96]{3,2,1,0:T(8,128)(2,1)S(1)} %get-tuple-element.97), channel_id=1, source_target_pairs={{0,16},{16,32},{32,48},{48,64},{64,80},{80,96},{96,112},{112,128},... | collective-permute-start | bytes 36872 | tf_op jit(solution)/shard_map/ppermute | solution.py:29
  18.4 2.4 copy-start
  19.5 13.8 %collective-permute-start.6 = (f32[1,9,8,96]{3,2,1,0:T(8,128)S(1)}, f32[1,9,8,96]{3,2,1,0:T(8,128)S(1)}, u32[]{:S(2)}, u32[]{:S(2)}) collective-permute-start(f32[1,9,8,96]{3,2,1,0:T(8,128)S(1)} %slice.1024), channel_id=1, source_target_pairs={{16,0},{32,16},{48,32},{64,48},{80,64},{96,80},{112,96},{128,112},... | collective-permute-start | bytes 82952 | tf_op jit(solution)/shard_map/ppermute | solution.py:38
  21.0 9.9 %collective-permute-start.3 = (bf16[10,1,8,96]{3,2,1,0:T(8,128)(2,1)S(1)}, bf16[10,1,8,96]{3,2,1,0:T(8,128)(2,1)S(1)}, u32[]{:S(2)}, u32[]{:S(2)}) collective-permute-start(bf16[10,1,8,96]{3,2,1,0:T(8,128)(2,1)S(1)} %get-tuple-element.90), channel_id=1, source_target_pairs={{1,0},{2,1},{3,2},{4,3},{5,4},{6,5},{7,6},{8,7},{9,8},{10,9},{11,1... | collective-permute-start | bytes 46088 | tf_op jit(solution)/shard_map/ppermute | solution.py:30
  28.9 3.1 collective-permute-start.2
  33.4 7.9 %collective-permute-start.7 = (f32[8,1,8,96]{3,2,1,0:T(8,128)S(1)}, f32[8,1,8,96]{3,2,1,0:T(8,128)S(1)}, u32[]{:S(2)}, u32[]{:S(2)}) collective-permute-start(f32[8,1,8,96]{3,2,1,0:T(8,128)S(1)} %pad_maximum_fusion.7), channel_id=1, source_target_pairs={{1,0},{2,1},{3,2},{4,3},{5,4},{6,5},{7,6},{8,7},{9,8},{10,9},{11,1... | collective-permute-start | bytes 73736 | tf_op jit(solution)/shard_map/ppermute | solution.py:38
  40.7 0.8 copy-start.4
  40.7 0.9 copy-start.6
  40.7 0.9 copy-start.39
  42.7 104.9 %collective-permute-start.4 = (bf16[1,8,8,96]{3,2,1,0:T(8,128)(2,1)S(1)}, bf16[1,8,8,96]{3,2,1,0:T(8,128)(2,1)S(1)}, u32[]{:S(2)}, u32[]{:S(2)}) collective-permute-start(bf16[1,8,8,96]{3,2,1,0:T(8,128)(2,1)S(1)} %slice.994), channel_id=1, source_target_pairs={{0,16},{16,32},{32,48},{48,64},{64,80},{80,96},{96,112},{112,128},... | collective-permute-start | bytes 36872 | tf_op jit(solution)/shard_map/ppermute | solution.py:38
  46.9 104.2 %collective-permute-start.9 = (bf16[1,8,8,96]{3,2,1,0:T(8,128)(2,1)S(1)}, bf16[1,8,8,96]{3,2,1,0:T(8,128)(2,1)S(1)}, u32[]{:S(2)}, u32[]{:S(2)}) collective-permute-start(bf16[1,8,8,96]{3,2,1,0:T(8,128)(2,1)S(1)} %get-tuple-element.94), channel_id=1, source_target_pairs={{16,0},{32,16},{48,32},{64,48},{80,64},{96,80},{112,96},{128,112},... | collective-permute-start | bytes 36872 | tf_op jit(solution)/shard_map/ppermute | solution.py:30
  48.2 102.9 %collective-permute-start.8 = (bf16[1,8,8,96]{3,2,1,0:T(8,128)(2,1)S(1)}, bf16[1,8,8,96]{3,2,1,0:T(8,128)(2,1)S(1)}, u32[]{:S(2)}, u32[]{:S(2)}) collective-permute-start(bf16[1,8,8,96]{3,2,1,0:T(8,128)(2,1)S(1)} %get-tuple-element.93), channel_id=1, source_target_pairs={{0,16},{16,32},{32,48},{48,64},{64,80},{80,96},{96,112},{112,128},... | collective-permute-start | bytes 36872 | tf_op jit(solution)/shard_map/ppermute | solution.py:29
  71.1 13.7 %all-to-all-start.4 = ((f32[16,32,1]{1,2,0:T(1,128)}), f32[16,32,1]{1,2,0:T(1,128)S(1)}, u32[]{:S(2)}, u32[]{:S(2)}) async-start(f32[16,32,1]{1,2,0:T(1,128)} %copy.263), calls=%async_computation.4 | async-start | bytes 16384 | tf_op jit(solution)/shard_map/all_to_all | solution.py:49
  85.6 26.7 %all-to-all-start.5 = ((f32[32,1,1]{2,1,0:T(1,128)}), f32[32,1,1]{2,1,0:T(1,128)S(1)}, u32[]{:S(2)}, u32[]{:S(2)}) async-start(f32[32,1,1]{2,1,0:T(1,128)} %copy.264), calls=%async_computation.5 | async-start | bytes 32768 | tf_op jit(solution)/shard_map/all_to_all | solution.py:57
  114.2 12.4 %all-to-all-start.6 = ((f32[32,1,1]{2,1,0:T(1,128)}), f32[32,1,1]{2,1,0:T(1,128)S(1)}, u32[]{:S(2)}, u32[]{:S(2)}) async-start(f32[32,1,1]{2,1,0:T(1,128)} %broadcast_in_dim.24), calls=%async_computation.6 | async-start | bytes 32768 | tf_op jit(solution)/shard_map/all_to_all | solution.py:70
  127.5 13.5 %all-to-all-start.7 = ((f32[16,32,1]{1,2,0:T(1,128)}), f32[16,32,1]{1,2,0:T(1,128)S(1)}, u32[]{:S(2)}, u32[]{:S(2)}) async-start(f32[16,32,1]{1,2,0:T(1,128)} %broadcast_in_dim.25), calls=%async_computation.7 | async-start | bytes 16384 | tf_op jit(solution)/shard_map/all_to_all | solution.py:70
  141.0 106.2 %all-to-all-start = ((f32[16,32,486]{2,1,0:T(8,128)}), f32[16,32,486]{2,1,0:T(8,128)S(1)}, u32[]{:S(2)}, u32[]{:S(2)}) async-start(f32[16,32,486]{2,1,0:T(8,128)} %bitcast.1033), calls=%async_computation | async-start | bytes 2097152 | tf_op jit(solution)/shard_map/all_to_all | solution.py:49
  146.9 79.2 %copy-start.1 = (bf16[27,96,96]{2,1,0:T(8,128)(2,1)S(1)}, bf16[27,96,96]{2,1,0:T(8,128)(2,1)}, u32[]{:S(2)}) copy-start(bf16[27,96,96]{2,1,0:T(8,128)(2,1)} %param.10) | copy-start | bytes 1492996
  147.6 22.3 %collective-permute-start.5 = (bf16[9,1,8,96]{3,2,1,0:T(8,128)(2,1)S(1)}, bf16[9,1,8,96]{3,2,1,0:T(8,128)(2,1)S(1)}, u32[]{:S(2)}, u32[]{:S(2)}) collective-permute-start(bf16[9,1,8,96]{3,2,1,0:T(8,128)(2,1)S(1)} %pad_maximum_fusion.14), channel_id=1, source_target_pairs={{0,1},{1,2},{2,3},{3,4},{4,5},{5,6},{6,7},{7,8},{8,9},{9,10},{10,1... | collective-permute-start | bytes 41480 | tf_op jit(solution)/shard_map/ppermute | solution.py:38
  151.8 92.6 %collective-permute-start.11 = (bf16[10,1,8,96]{3,2,1,0:T(8,128)(2,1)}, bf16[10,1,8,96]{3,2,1,0:T(8,128)(2,1)S(1)}, u32[]{:S(2)}, u32[]{:S(2)}) collective-permute-start(bf16[10,1,8,96]{3,2,1,0:T(8,128)(2,1)} %get-tuple-element.86), channel_id=1, source_target_pairs={{1,0},{2,1},{3,2},{4,3},{5,4},{6,5},{7,6},{8,7},{9,8},{10,9},{11,1... | collective-permute-start | bytes 46088 | tf_op jit(solution)/shard_map/ppermute | solution.py:30
  153.7 90.7 %collective-permute-start.10 = (bf16[10,1,8,96]{3,2,1,0:T(8,128)(2,1)}, bf16[10,1,8,96]{3,2,1,0:T(8,128)(2,1)S(1)}, u32[]{:S(2)}, u32[]{:S(2)}) collective-permute-start(bf16[10,1,8,96]{3,2,1,0:T(8,128)(2,1)} %get-tuple-element.85), channel_id=1, source_target_pairs={{0,1},{1,2},{2,3},{3,4},{4,5},{5,6},{6,7},{7,8},{8,9},{9,10},{10,1... | collective-permute-start | bytes 46088 | tf_op jit(solution)/shard_map/ppermute | solution.py:29
  170.8 55.6 %copy-start.37 = (bf16[4,4,4,96]{3,2,1,0:T(4,128)(2,1)}, bf16[4,4,4,96]{3,2,1,0:T(4,128)(2,1)S(1)}, u32[]{:S(2)}) copy-start(bf16[4,4,4,96]{3,2,1,0:T(4,128)(2,1)S(1)} %slice.817) | copy-start | bytes 36868
  225.8 3.3 copy-start.36
  225.8 3.6 copy-start.35
  225.8 4.9 %copy-start.34 = (bf16[4,4,4,96]{3,2,1,0:T(4,128)(2,1)S(1)}, bf16[4,4,4,96]{3,2,1,0:T(4,128)(2,1)}, u32[]{:S(2)}) copy-start(bf16[4,4,4,96]{3,2,1,0:T(4,128)(2,1)} %slice.825) | copy-start | bytes 36868
  225.9 5.0 %copy-start.33 = (bf16[4,4,4,96]{3,2,1,0:T(4,128)(2,1)S(1)}, bf16[4,4,4,96]{3,2,1,0:T(4,128)(2,1)}, u32[]{:S(2)}) copy-start(bf16[4,4,4,96]{3,2,1,0:T(4,128)(2,1)} %slice.827) | copy-start | bytes 36868
  226.2 5.0 %copy-start.32 = (bf16[4,4,4,96]{3,2,1,0:T(4,128)(2,1)S(1)}, bf16[4,4,4,96]{3,2,1,0:T(4,128)(2,1)}, u32[]{:S(2)}) copy-start(bf16[4,4,4,96]{3,2,1,0:T(4,128)(2,1)} %slice.829) | copy-start | bytes 36868
  227.3 4.3 %copy-start.31 = (bf16[4,4,4,96]{3,2,1,0:T(4,128)(2,1)S(1)}, bf16[4,4,4,96]{3,2,1,0:T(4,128)(2,1)}, u32[]{:S(2)}) copy-start(bf16[4,4,4,96]{3,2,1,0:T(4,128)(2,1)} %slice.831) | copy-start | bytes 36868
  229.1 2.8 copy-start.30
  229.4 2.9 copy-start.29
  229.8 2.9 copy-start.28
  238.0 1.1 copy-start.2
  247.2 36.6 %all-to-all-start.8 = ((f32[16,32,486]{2,1,0:T(8,128)}), f32[16,32,486]{2,1,0:T(8,128)S(1)}, u32[]{:S(2)}, u32[]{:S(2)}) async-start(f32[16,32,486]{2,1,0:T(8,128)} %bitcast.1032), calls=%async_computation.8 | async-start | bytes 2097152 | tf_op jit(solution)/shard_map/all_to_all | solution.py:49
  255.8 3.0 copy-start.22
  255.8 3.2 copy-start.21
  255.8 3.4 copy-start.23
  257.7 1.7 copy-start.20
  259.4 28.2 %copy-start.19 = (bf16[8,8,8,96]{3,2,1,0:T(8,128)(2,1)S(1)}, bf16[8,8,8,96]{3,2,1,0:T(8,128)(2,1)}, u32[]{:S(2)}) copy-start(bf16[8,8,8,96]{3,2,1,0:T(8,128)(2,1)} %get-tuple-element.44) | copy-start | bytes 294916
  260.5 39.8 %copy-start.18 = (bf16[8,8,8,96]{3,2,1,0:T(8,128)(2,1)S(1)}, bf16[8,8,8,96]{3,2,1,0:T(8,128)(2,1)}, u32[]{:S(2)}) copy-start(bf16[8,8,8,96]{3,2,1,0:T(8,128)(2,1)} %get-tuple-element.43) | copy-start | bytes 294916
  283.7 12.7 %all-to-all-start.1 = ((f32[32,1,486]{2,1,0:T(1,128)}), f32[32,1,486]{2,1,0:T(1,128)S(1)}, u32[]{:S(2)}, u32[]{:S(2)}) async-start(f32[32,1,486]{2,1,0:T(1,128)} %all_to_all.55), calls=%async_computation.1 | async-start | bytes 131072 | tf_op jit(solution)/shard_map/all_to_all | solution.py:57
  287.6 26.1 %copy-start.27 = (bf16[8,8,8,96]{3,2,1,0:T(8,128)(2,1)S(1)}, bf16[8,8,8,96]{3,2,1,0:T(8,128)(2,1)}, u32[]{:S(2)}) copy-start(bf16[8,8,8,96]{3,2,1,0:T(8,128)(2,1)} %get-tuple-element.75) | copy-start | bytes 294916
  287.8 39.5 %copy-start.17 = (bf16[8,8,8,96]{3,2,1,0:T(8,128)(2,1)S(1)}, bf16[8,8,8,96]{3,2,1,0:T(8,128)(2,1)}, u32[]{:S(2)}) copy-start(bf16[8,8,8,96]{3,2,1,0:T(8,128)(2,1)} %get-tuple-element.42) | copy-start | bytes 294916
  296.5 12.7 %all-to-all-start.9 = ((f32[32,1,486]{2,1,0:T(1,128)}), f32[32,1,486]{2,1,0:T(1,128)S(1)}, u32[]{:S(2)}, u32[]{:S(2)}) async-start(f32[32,1,486]{2,1,0:T(1,128)} %all_to_all.67), calls=%async_computation.9 | async-start | bytes 131072 | tf_op jit(solution)/shard_map/all_to_all | solution.py:57
  309.8 12.7 %all-to-all-start.2 = ((f32[32,1,486]{2,1,0:T(1,128)}), f32[32,1,486]{2,1,0:T(1,128)S(1)}, u32[]{:S(2)}, u32[]{:S(2)}) async-start(f32[32,1,486]{2,1,0:T(1,128)} %broadcast_in_dim.22), calls=%async_computation.2 | async-start | bytes 131072 | tf_op jit(solution)/shard_map/all_to_all | solution.py:70
  323.2 12.7 %all-to-all-start.10 = ((f32[32,1,486]{2,1,0:T(1,128)}), f32[32,1,486]{2,1,0:T(1,128)S(1)}, u32[]{:S(2)}, u32[]{:S(2)}) async-start(f32[32,1,486]{2,1,0:T(1,128)} %broadcast_in_dim.26), calls=%async_computation.10 | async-start | bytes 131072 | tf_op jit(solution)/shard_map/all_to_all | solution.py:70
  337.1 8.4 %copy-start.5 = (f32[512,96]{0,1:T(8,128)S(1)}, f32[512,96]{0,1:T(8,128)}, u32[]{:S(2)}) copy-start(f32[512,96]{0,1:T(8,128)} %fusion.82) | copy-start | bytes 589828
  337.1 8.4 %copy-start.16 = (bf16[8,8,8,96]{3,2,1,0:T(8,128)(2,1)S(1)}, bf16[8,8,8,96]{3,2,1,0:T(8,128)(2,1)}, u32[]{:S(2)}) copy-start(bf16[8,8,8,96]{3,2,1,0:T(8,128)(2,1)} %get-tuple-element.41) | copy-start | bytes 294916
  337.1 8.6 %copy-start.15 = (bf16[8,8,8,96]{3,2,1,0:T(8,128)(2,1)S(1)}, bf16[8,8,8,96]{3,2,1,0:T(8,128)(2,1)}, u32[]{:S(2)}) copy-start(bf16[8,8,8,96]{3,2,1,0:T(8,128)(2,1)} %get-tuple-element.40) | copy-start | bytes 294916
  337.1 8.8 %copy-start.14 = (bf16[8,8,8,96]{3,2,1,0:T(8,128)(2,1)S(1)}, bf16[8,8,8,96]{3,2,1,0:T(8,128)(2,1)}, u32[]{:S(2)}) copy-start(bf16[8,8,8,96]{3,2,1,0:T(8,128)(2,1)} %get-tuple-element.39) | copy-start | bytes 294916
  337.1 36.3 %all-to-all-start.3 = ((f32[16,32,486]{2,1,0:T(8,128)}), f32[16,32,486]{2,1,0:T(8,128)S(1)}, u32[]{:S(2)}, u32[]{:S(2)}) async-start(f32[16,32,486]{2,1,0:T(8,128)} %broadcast_in_dim.23), calls=%async_computation.3 | async-start | bytes 2097152 | tf_op jit(solution)/shard_map/all_to_all | solution.py:70
  345.4 0.9 copy-start.26
  345.4 1.1 copy-start.13
  345.5 1.2 copy-start.12
  345.7 1.2 copy-start.25
  345.9 1.2 copy-start.11
  374.5 3.7 copy-start.10
  374.5 3.9 copy-start.9
  374.5 31.6 %all-to-all-start.11 = ((f32[16,32,486]{2,1,0:T(8,128)}), f32[16,32,486]{2,1,0:T(8,128)S(1)}, u32[]{:S(2)}, u32[]{:S(2)}) async-start(f32[16,32,486]{2,1,0:T(8,128)} %broadcast_in_dim.27), calls=%async_computation.11 | async-start | bytes 2097152 | tf_op jit(solution)/shard_map/all_to_all | solution.py:70
  378.2 1.5 copy-start.8
  378.2 1.7 copy-start.24
  378.2 1.9 copy-start.7
where the time goes:
time: 411 us; the launch traced here: 409 us
  waiting for transfers between devices  137 us (33%)
  starting transfers between devices  116 us (28%)
  local copies, waits for them, and re-layouts  91.4 us (22%)
  matrix products  54.7 us (13%)
  other arithmetic  8 us (2%)
    all_to_all x6, waiting for transfers between devices, from_everyone(): return lax.all_to_all(copies, axis, split_axis=0, concat_axis=0, tiled=True)  73.7 us
    slice x27, local copies, waits for them, and re-layouts, stride_window(): lax.slice(padded, (1 + step_x, 1 + step_y, 1 + step_z, 0), (2 + step_x +...  55.7 us
    all_to_all x6, starting transfers between devices, from_everyone(): return lax.all_to_all(copies, axis, split_axis=0, concat_axis=0, tiled=True)  30.3 us
    all_to_all x3, waiting for transfers between devices, sent_and_summed(): lax.all_to_all(blocks, axis, split_axis=0, concat_axis=0, tiled=True)  26.1 us
    all_to_all x3, starting transfers between devices, sum_by_axis(): lax.all_to_all(nearer, far, split_axis=0, concat_axis=0, tiled=True)  25.9 us
    all_to_all x3, waiting for transfers between devices, sum_by_axis(): lax.all_to_all(nearer, far, split_axis=0, concat_axis=0, tiled=True)  24.2 us
    dot_general x27, matrix products, weight_taps(): jnp.dot(window.reshape(-1, channels).T, flat_grad, preferred_element_type...  22.8 us
    all_to_all x3, starting transfers between devices, sent_and_summed(): lax.all_to_all(blocks, axis, split_axis=0, concat_axis=0, tiled=True)  21.3 us
  transfers between devices with their start and end apart: 24, of which 13 were waited for; matrix products, arithmetic and copies ran while one was open for 34% of the time, Pallas kernels for 0%

commit v1 on v0

v1 whole, which is shorter than its diff:
```python
import math

import jax
import jax.numpy as jnp
from jax import lax
from jax.experimental import pallas as pl
from jax.experimental.pallas import tpu as pltpu
from jax.sharding import PartitionSpec as P

F32 = jnp.float32
BF16 = jnp.bfloat16
MESH = pl.DeviceIdType.MESH

C = 96
LANES = 128
TAPS = 27
TILE = 8
HALF = 4
DEEP = 8
K_ALL = TAPS * LANES
ROWS = 2048
NX, NY, NZ = 4, 8, 8
TAP_OFFSETS = [(a, b, e) for a in (-1, 0, 1) for b in (-1, 0, 1) for e in (-1, 0, 1)]

SIDES = [(-1, 0), (1, 0), (0, -1), (0, 1), (-1, -1), (-1, 1), (1, -1), (1, 1)]
SIDE_ROWS = [160 if 0 in side else 48 for side in SIDES]
SIDE_AT = [sum(SIDE_ROWS[:i]) for i in range(8)]
HALO_ROWS = sum(SIDE_ROWS)

PIECES = [
    (0, 1, 8, 1, 8),
    (512, 0, 1, 0, 10),
    (592, 9, 1, 0, 10),
    (672, 1, 8, 0, 1),
    (736, 1, 8, 9, 1),
]


def edge(step, length, width):
    return {-1: (0, width), 0: (0, length), 1: (length - width, width)}[step]


def landing(step, length, width):
    return {-1: (0, width), 0: (width, length), 1: (width + length, width)}[step]


def dot(left, right):
    return lax.dot_general(left, right, (((1,), (0,)), ((), ())), preferred_element_type=F32)


def dot_nt(left, right):
    return lax.dot_general(left, right, (((1,), (1,)), ((), ())), preferred_element_type=F32)


def iota(shape, dim):
    return lax.broadcasted_iota(jnp.int32, shape, dim)


def z_shifts(value):
    columns = value.shape[0]
    level = iota((columns, DEEP, LANES), 1)
    below = jnp.where(level == 0, 0.0, pltpu.roll(value, 1, 1))
    above = jnp.where(level == DEEP - 1, 0.0, pltpu.roll(value, DEEP - 1, 1))
    return below, value, above


def store_shifts(ref, value, at_x, size_x, at_y, size_y):
    for k, shifted in enumerate(z_shifts(value.reshape(size_x * size_y, DEEP, LANES))):
        ref[k, at_x : at_x + size_x, at_y : at_y + size_y] = shifted.reshape(
            size_x, size_y, DEEP, LANES
        )


def dense_tiles(acc, extra):
    lane = iota((C, LANES), 1)
    tap = lambda t: acc[:, t * LANES : (t + 1) * LANES]
    tiles = []
    for group in range(7):
        first = 4 * group
        one = pltpu.roll(tap(first + 1), 96, 1)
        two = pltpu.roll(tap(first + 2), 64, 1)
        tiles.append(jnp.where(lane < 96, tap(first), one))
        tiles.append(jnp.where(lane < 64, one, two))
        if group < 6:
            three = pltpu.roll(tap(first + 3), 32, 1)
        else:
            three = jnp.where(lane == 32, pltpu.roll(extra, 64, 1), 0.0)
        tiles.append(jnp.where(lane < 32, two, three))
    return tiles


def main_kernel(
    vox_ref, occ_ref, cw_ref, bias_ref, dw_ref, cot_ref,
    fin_ref, down_ref, gv_ref,
    hs, hr, a3, c3, gs10, s3, g3, pre, p1, p2, ps, wf, wb, df, db, cl,
    part, rc, xs, xr, ys, yr, zs, zr, zg,
    h_send, h_recv, c_send, c_recv, x_send, x_recv, y_send, y_recv, z_send, z_recv,
    zg_send, zg_recv, yg_send, yg_recv, xg_send, xg_recv, cg_send, cg_recv,
):
    gx = lax.axis_index("gx")
    gy = lax.axis_index("gy")
    n_gx = lax.axis_size("gx")
    n_gy = lax.axis_size("gy")
    px, pz = gx // NZ, gx % NZ
    py, core = gy // 2, gy % 2
    sibling = (gx, gy + 1 - 2 * core)
    side_peer = [((gx + sx + n_gx) % n_gx, (gy + sy + n_gy) % n_gy) for sx, sy in SIDES]
    x_peer = [(((px + k) % NX) * NZ + pz, gy) for k in range(NX)]
    y_peer = [(gx, ((py + k) % NY) * 2 + core) for k in range(NY)]
    z_peer = [(px * NZ + (pz + k) % NZ, gy) for k in range(NZ)]

    def chosen(first, second):
        return tuple(i + core * (j - i) for i, j in zip(first, second))

    near = [chosen(y_peer[k], z_peer[k]) for k in range(8)]
    far = [chosen(z_peer[k], y_peer[k]) for k in range(8)]
    i_near = py + core * (pz - py)
    i_far = pz + core * (py - pz)

    barrier = pltpu.get_barrier_semaphore()
    greeted = side_peer + [sibling] + x_peer[1:] + y_peer[1:] + z_peer[1:]
    for peer in greeted:
        pl.semaphore_signal(barrier, inc=1, device_id=peer, device_id_type=MESH)

    def remote(src, dst, send, recv, peer):
        return pltpu.make_async_remote_copy(
            src_ref=src, dst_ref=dst, send_sem=send, recv_sem=recv, device_id=peer,
            device_id_type=MESH,
        )

    spread = (iota((512, 64), 0) // DEEP == iota((512, 64), 1)).astype(BF16)
    by_column = dot(spread, occ_ref[...].astype(F32).astype(BF16))
    own_level = iota((512, DEEP), 0) % DEEP == iota((512, DEEP), 1)
    picked = jnp.where(own_level, by_column, 0.0).astype(BF16)
    live = dot(picked, jnp.ones((DEEP, LANES), BF16))
    widen = (iota((C, LANES), 0) == iota((C, LANES), 1)).astype(BF16)
    lane512 = iota((512, LANES), 1)
    masked = jnp.where(lane512 == C, live, dot(vox_ref[...], widen) * live)
    masked = masked.reshape(TILE, TILE, DEEP, LANES)
    pairs = live.reshape(HALF, 2, HALF, 2, DEEP, LANES)
    most = jnp.maximum(
        jnp.maximum(pairs[:, 0, :, 0], pairs[:, 0, :, 1]),
        jnp.maximum(pairs[:, 1, :, 0], pairs[:, 1, :, 1]),
    ).reshape(HALF * HALF, DEEP, LANES)
    coarse_live = jnp.maximum(most, pltpu.roll(most, DEEP - 1, 1)).reshape(128, LANES)
    cl[...] = coarse_live
    upward = (iota((128, 64), 0) == 2 * iota((128, 64), 1)).astype(BF16)
    cot = (dot(upward, dot(cot_ref[...], widen).astype(BF16)) * coarse_live).reshape(
        HALF, HALF, DEEP, LANES
    )

    for i, (sx, sy) in enumerate(SIDES):
        x0, wx = edge(sx, TILE, 2)
        y0, wy = edge(sy, TILE, 2)
        rows = wx * wy * DEEP
        at = SIDE_AT[i]
        hs[at : at + rows, :] = (
            masked[x0 : x0 + wx, y0 : y0 + wy].reshape(rows, LANES).astype(BF16)
        )
        x0, wx = edge(sx, HALF, 1)
        y0, wy = edge(sy, HALF, 1)
        more = wx * wy * DEEP
        block = cot[x0 : x0 + wx, y0 : y0 + wy].reshape(more, LANES)
        if more < 16:
            block = jnp.concatenate([block, jnp.zeros((16 - more, LANES), F32)], 0)
        hs[at + rows : at + SIDE_ROWS[i], :] = block.astype(BF16)

    pl.semaphore_wait(barrier, len(greeted))
    halo = []
    for i, (sx, sy) in enumerate(SIDES):
        there = SIDES.index((-sx, -sy))
        mine = pl.ds(SIDE_AT[i], SIDE_ROWS[i])
        theirs = pl.ds(SIDE_AT[there], SIDE_ROWS[i])
        copy = remote(hs.at[mine], hr.at[theirs], h_send.at[i], h_recv.at[there], side_peer[i])
        copy.start()
        halo.append(copy)

    store_shifts(a3, masked, 2, TILE, 2, TILE)
    store_shifts(c3, cot, 1, HALF, 1, HALF)
    for ref in (wf, wb, df, db):
        ref[...] = jnp.zeros(ref.shape, BF16)
    for t in range(TAPS):
        for source, plain, turned in ((cw_ref, wf, wb), (dw_ref, df, db)):
            block = source[t]
            plain[t * LANES : t * LANES + C, 0:C] = block
            turned[0:C, t * LANES : t * LANES + C] = block
    for w in (0, 1):
        part[w, 2016:2048, :] = jnp.zeros((32, LANES), BF16)

    for copy in halo:
        copy.wait()
    for i, (sx, sy) in enumerate(SIDES):
        inside = 1.0
        for step, at, size in ((sx, gx, n_gx), (sy, gy, n_gy)):
            if step:
                inside = inside * jnp.where(at == (0 if step < 0 else size - 1), 0.0, 1.0)
        at = SIDE_AT[i]
        x0, wx = landing(sx, TILE, 2)
        y0, wy = landing(sy, TILE, 2)
        rows = wx * wy * DEEP
        store_shifts(a3, hr[at : at + rows, :].astype(F32) * inside, x0, wx, y0, wy)
        x0, wx = landing(sx, HALF, 1)
        y0, wy = landing(sy, HALF, 1)
        more = wx * wy * DEEP
        block = hr[at + rows : at + SIDE_ROWS[i], :].astype(F32)[:more] * inside
        store_shifts(c3, block, x0, wx, y0, wy)

    for t, (a, b, e) in enumerate(TAP_OFFSETS):
        lanes = slice(t * LANES, (t + 1) * LANES)
        for row, x0, wx, y0, wy in PIECES:
            x1, y1 = x0 + 1 + a, y0 + 1 + b
            rows = wx * wy * DEEP
            window = a3[e + 1, x1 : x1 + wx, y1 : y1 + wy]
            p1[row : row + rows, lanes] = window.reshape(rows, LANES).astype(BF16)
    pre[...] = dot(p1[...], wf[...]) + bias_ref[...]

    for parity_x in (0, 1):
        for parity_y in (0, 1):
            total = None
            for a in ((-1, 1) if parity_x else (0,)):
                for b in ((-1, 1) if parity_y else (0,)):
                    x0 = 0 if a == 1 else 1
                    y0 = 0 if b == 1 else 1
                    windows = [
                        c3[1 - e, x0 : x0 + 5, y0 : y0 + 5].reshape(200, LANES).astype(BF16)
                        for e in (-1, 0, 1)
                    ]
                    t = 9 * (a + 1) + 3 * (b + 1)
                    term = dot_nt(
                        jnp.concatenate(windows, 1), db[:, t * LANES : (t + 3) * LANES]
                    )
                    total = term if total is None else total + term
            gs10[:, 1 - parity_x, :, 1 - parity_y] = total.reshape(5, 5, DEEP, LANES)

    pick_live = (iota((LANES, LANES), 0) == C).astype(BF16)
    ten = gs10.reshape(10, 10, DEEP, LANES)
    for row, x0, wx, y0, wy in PIECES:
        rows = wx * wy * DEEP
        value = pre[row : row + rows, :]
        feature = p1[row : row + rows, 13 * LANES : 14 * LANES]
        alive = dot(feature, pick_live)
        gate = 1.0 / (1.0 + jnp.exp(-value))
        summed = (feature.astype(F32) + alive * (value * gate)).astype(BF16).astype(F32)
        grad_sum = ten[x0 : x0 + wx, y0 : y0 + wy].reshape(rows, LANES)
        grad_pre = grad_sum * alive * gate * (1.0 + value * (1.0 - gate))
        store_shifts(s3, summed, x0, wx, y0, wy)
        store_shifts(g3, grad_pre.astype(BF16).astype(F32), x0, wx, y0, wy)

    six = s3.reshape(3, 5, 2, 5, 2, DEEP, LANES)
    for t, (a, b, e) in enumerate(TAP_OFFSETS):
        i0, si = (a + 1) // 2, (a + 1) % 2
        j0, sj = (b + 1) // 2, (b + 1) % 2
        window = six[e + 1, i0 : i0 + 4, si, j0 : j0 + 4, sj]
        ps[:, t * LANES : (t + 1) * LANES] = window.reshape(128, LANES).astype(BF16)
    cot_turned = c3[1, 1:5, 1:5].reshape(128, LANES).T[0:C].astype(BF16)
    acc = dot(cot_turned, ps[...])
    for j, tile in enumerate(dense_tiles(acc, jnp.zeros((C, LANES), F32))):
        part[1, j * C : (j + 1) * C, :] = tile.astype(BF16)

    order = (2, 1, 3, 0)
    chunk = [pl.ds(pl.multiple_of(((px + k) % NX) * 512, 512), 512) for k in range(NX)]
    core_copies = [
        remote(part.at[1 - core, chunk[k]], rc.at[chunk[k]], c_send.at[k], c_recv.at[k], sibling)
        for k in range(NX)
    ]

    @pl.when(core == 0)
    def _():
        for k in order:
            core_copies[k].start()

    pre_turned = g3[1, 1:9, 1:9].reshape(512, LANES).T[0:C].astype(BF16)
    acc = dot(pre_turned, p1[0:512, :])
    for j, tile in enumerate(dense_tiles(acc, acc[:, 13 * LANES : 14 * LANES])):
        part[0, j * C : (j + 1) * C, :] = tile.astype(BF16)

    @pl.when(core == 1)
    def _():
        for k in order:
            core_copies[k].start()

    downward = (iota((64, 128), 1) == 2 * iota((64, 128), 0)).astype(BF16)
    coarse = (dot(ps[...], df[...]) * cl[...]).astype(BF16)
    down_ref[...] = dot(downward, coarse).astype(BF16)

    x_copies = []
    for k in order:
        core_copies[k].wait()
        both = part[core, chunk[k]].astype(F32) + rc[chunk[k]].astype(F32)
        xs[k] = both.astype(BF16)
        if k:
            copy = remote(xs.at[k], xr.at[k], x_send.at[k], x_recv.at[k], x_peer[k])
            copy.start()
            x_copies.append(copy)

    for t, (a, b, e) in enumerate(TAP_OFFSETS):
        window = g3[1 - e, 1 - a : 9 - a, 1 - b : 9 - b]
        p2[:, t * LANES : (t + 1) * LANES] = window.reshape(512, LANES).astype(BF16)
    grad_in = ten[1:9, 1:9].reshape(512, LANES) + dot_nt(p2[...], wb[...])
    alive = dot(p1[0:512, 13 * LANES : 14 * LANES], pick_live)
    gv_ref[...] = (grad_in * alive).astype(BF16)

    for copy in x_copies:
        copy.wait()
    ys[...] = (
        xs[0].astype(F32) + xr[1].astype(F32) + xr[2].astype(F32) + xr[3].astype(F32)
    ).astype(BF16).reshape(8, 64, LANES)
    copies = []
    for k in (4, 3, 5, 2, 6, 1, 7):
        block = ys.at[(i_near + k) % 8]
        copies.append(remote(block, yr.at[k], y_send.at[k], y_recv.at[k], near[k]))
        copies[-1].start()
    for copy in copies:
        copy.wait()
    total = ys[i_near].astype(F32)
    for k in range(1, 8):
        total = total + yr[k].astype(F32)
    zs[...] = total.reshape(8, 8, LANES)
    copies = []
    for k in (4, 3, 5, 2, 6, 1, 7):
        block = zs.at[(i_far + k) % 8]
        copies.append(remote(block, zr.at[k], z_send.at[k], z_recv.at[k], far[k]))
        copies[-1].start()
    for copy in copies:
        copy.wait()
    total = zs[i_far]
    for k in range(1, 8):
        total = total + zr[k]

    zg[i_far] = total
    copies = []
    for k in (4, 3, 5, 2, 6, 1, 7):
        block = zg.at[i_far]
        copies.append(remote(block, block, zg_send.at[k], zg_recv.at[k], far[k]))
        copies[-1].start()
    for copy in copies:
        copy.wait()
    own = pl.ds(pl.multiple_of(px * 512 + i_near * 64, 64), 64)
    fin_ref[core, own] = zg[...].reshape(64, LANES).astype(BF16)
    copies = []
    for k in (4, 3, 5, 2, 6, 1, 7):
        block = fin_ref.at[core, own]
        copies.append(remote(block, block, yg_send.at[k], yg_recv.at[k], near[k]))
        copies[-1].start()
    for copy in copies:
        copy.wait()
    copies = {}
    for k in (2, 1, 3):
        block = fin_ref.at[core, chunk[0]]
        copies[k] = remote(block, block, xg_send.at[k], xg_recv.at[k], x_peer[k])
        copies[k].start()
    last = []
    for k in (0, 1, 3, 2):
        if k:
            copies[k].wait()
        block = fin_ref.at[core, chunk[-k % NX]]
        last.append(remote(block, block, cg_send.at[k], cg_recv.at[k], sibling))
        last[-1].start()
    for copy in last:
        copy.wait()


def finish_kernel(factor, fin_ref, down_in, gv_in, down_ref, gv_ref, gc_ref, gb_ref, gd_ref):
    down_ref[...] = down_in[:, 0:C]
    gv_ref[...] = gv_in[:, 0:C]
    lane = iota((C, LANES), 1)
    for w, out in ((0, gc_ref), (1, gd_ref)):
        for group in range(7):
            first, second, third = (
                fin_ref[w, (3 * group + i) * C : (3 * group + i + 1) * C, :].astype(F32) * factor
                for i in range(3)
            )
            taps = [
                first,
                pltpu.roll(jnp.where(lane >= 96, first, second), 32, 1),
                pltpu.roll(jnp.where(lane >= 64, second, third), 64, 1),
                pltpu.roll(third, 96, 1),
            ]
            for i in range(4 if group < 6 else 3):
                out[4 * group + i] = taps[i].T[0:C]
        if w == 0:
            gb_ref[...] = third.T[32:33]


def on_device(voxels, occupancy, conv_weight, conv_bias, down_weight, down_cotangent):
    vmem = pl.BlockSpec(memory_space=pltpu.VMEM)
    bias = jnp.pad(conv_bias, (0, LANES - C)).reshape(1, LANES)
    scratch = [
        ((HALO_ROWS, LANES), BF16),
        ((HALO_ROWS, LANES), BF16),
        ((3, 12, 12, DEEP, LANES), F32),
        ((3, 6, 6, DEEP, LANES), F32),
        ((5, 2, 5, 2, DEEP, LANES), F32),
        ((3, 10, 10, DEEP, LANES), F32),
        ((3, 10, 10, DEEP, LANES), F32),
        ((800, LANES), F32),
        ((800, K_ALL), BF16),
        ((512, K_ALL), BF16),
        ((128, K_ALL), BF16),
        ((K_ALL, LANES), BF16),
        ((LANES, K_ALL), BF16),
        ((K_ALL, LANES), BF16),
        ((LANES, K_ALL), BF16),
        ((128, LANES), F32),
        ((2, ROWS, LANES), BF16),
        ((ROWS, LANES), BF16),
        ((4, 512, LANES), BF16),
        ((4, 512, LANES), BF16),
        ((8, 64, LANES), BF16),
        ((8, 64, LANES), BF16),
        ((8, 8, LANES), F32),
        ((8, 8, LANES), F32),
        ((8, 8, LANES), F32),
    ]
    semaphores = [8, 8, 4, 4, 4, 4, 8, 8, 8, 8, 8, 8, 8, 8, 4, 4, 4, 4]
    fin, down, grad_voxels = pl.pallas_call(
        main_kernel,
        out_shape=(
            jax.ShapeDtypeStruct((2, ROWS, LANES), BF16),
            jax.ShapeDtypeStruct((64, LANES), BF16),
            jax.ShapeDtypeStruct((512, LANES), BF16),
        ),
        in_specs=[vmem] * 6,
        out_specs=(vmem, vmem, vmem),
        scratch_shapes=[pltpu.VMEM(shape, dtype) for shape, dtype in scratch]
        + [pltpu.SemaphoreType.DMA((n,)) for n in semaphores],
        compiler_params=pltpu.CompilerParams(
            collective_id=0, has_side_effects=True, vmem_limit_bytes=56 * 1024 * 1024
        ),
    )(
        voxels.reshape(512, C),
        occupancy.reshape(64, DEEP),
        conv_weight,
        bias,
        down_weight,
        down_cotangent.reshape(64, C),
    )
    cells = voxels.shape[0] * lax.axis_size("gx") * voxels.shape[1] * lax.axis_size("gy") * DEEP
    factor = 1.0 / math.sqrt(cells)
    down, grad_voxels, grad_conv, grad_bias, grad_down = pl.pallas_call(
        lambda *refs: finish_kernel(factor, *refs),
        out_shape=(
            jax.ShapeDtypeStruct((64, C), BF16),
            jax.ShapeDtypeStruct((512, C), BF16),
            jax.ShapeDtypeStruct((TAPS, C, C), F32),
            jax.ShapeDtypeStruct((1, C), F32),
            jax.ShapeDtypeStruct((TAPS, C, C), F32),
        ),
        in_specs=[vmem] * 3,
        out_specs=(vmem,) * 5,
        compiler_params=pltpu.CompilerParams(vmem_limit_bytes=32 * 1024 * 1024),
    )(fin, down, grad_voxels)
    return (
        down.reshape(down_cotangent.shape),
        grad_voxels.reshape(voxels.shape),
        grad_conv,
        grad_bias.reshape(C),
        grad_down,
    )


def solution(mesh):
    tile = P("gx", "gy", None, None)
    return jax.shard_map(
        on_device,
        mesh=mesh,
        in_specs=(tile, P("gx", "gy", None), P(), P(), P(), tile),
        out_specs=(tile, tile, P(), P(), P()),
        check_vma=False,
    )
```

time: 411 us -> 72.1 us (0.18)
  waiting for transfers between devices: 137 us -> 0 us
  starting transfers between devices: 116 us -> 0 us
  local copies, waits for them, and re-layouts: 91.4 us -> 4.01 us
  Pallas kernels: 0 us -> 67.2 us
  matrix products: 54.7 us -> 0 us
  other arithmetic: 8 us -> 0 us
    all_to_all x12 -> x0, waiting for transfers between devices: 124 us -> none  [the longest x6 73.7 us: from_everyone(): return lax.all_to_all(copies, axis, split_axis=0, concat_axis=0, tiled=True)]
    all_to_all x12 -> x0, starting transfers between devices: 77.4 us -> none  [the longest x6 30.3 us: from_everyone(): return lax.all_to_all(copies, axis, split_axis=0, concat_axis=0, tiled=True)]
    pallas_call x0 -> x2, Pallas kernels: none -> 67.2 us  [the longest x1 64.4 us: on_device(): pl.pallas_call(main_kernel, out_shape=(jax.ShapeDtypeStruct((2, ROWS, LAN...]
    slice x46 -> x0, local copies, waits for them, and re-layouts: 59.4 us -> none  [the longest x27 55.7 us: stride_window(): lax.slice(padded, (1 + step_x, 1 + step_y, 1 + step_z, 0), (2 + step_x +...]
    dot_general x162 -> x0, matrix products: 54.7 us -> none  [the longest x27 22.8 us: weight_taps(): jnp.dot(window.reshape(-1, channels).T, flat_grad, preferred_element_type...]
    ppermute x12 -> x0, starting transfers between devices: 38.5 us -> none  [the longest x4 15 us: with_halo(): before = lax.ppermute(last, axis, up)]
    ppermute x12 -> x0, waiting for transfers between devices: 12.9 us -> none  [the longest x4 11.8 us: from_behind(): return lax.ppermute(block, axis, route)]
    another operation x13 -> x0, local copies, waits for them, and re-layouts: 9.76 us -> none  [the longest x5 9.56 us: cut_along(): value.reshape(*dims[:dim], peers, dims[dim] // peers, *dims[dim + 1:])]
  transfers between devices with their start and end apart: 24 -> 0, of which waited for: 13 -> 0; matrix products, arithmetic and copies ran while one was open for 34% -> 0% of each run, Pallas kernels for 0% -> 0%
where the time goes in v1:
time: 72.1 us; the launch traced here: 71.9 us
  Pallas kernels  67.2 us (93%)
  local copies, waits for them, and re-layouts  4.01 us (6%)
    pallas_call x1, Pallas kernels, on_device(): pl.pallas_call(main_kernel, out_shape=(jax.ShapeDtypeStruct((2, ROWS, LAN...  64.4 us
    unnamed x6, local copies, waits for them, and re-layouts  2.84 us
    pallas_call x1, Pallas kernels, on_device(): pl.pallas_call(lambda *refs: finish_kernel(factor, *refs), out_shape=(jax...  2.78 us

profile of v1, /device:TPU:1, one launch (start us, length us, event | category | flops | bytes accessed | tf_op | source)
XLA Modules:
  0.0 71.9 jit_solution(3822524572064928975)
XLA Ops:
  0.6 1.2 %pad_bitcast_fusion.bias_ref = f32[1,128]{1,0:T(1,128)} fusion(f32[96]{0:T(128)} %param.9), kind=kLoop, calls=%fused_computation | loop fusion | bytes 896 | tf_op jit(solution)/shard_map/reshape | solution.py:387
  1.8 64.4 %shard_map.101 = (bf16[2,2048,128]{2,1,0:T(8,128)(2,1)}, bf16[64,128]{1,0:T(8,128)(2,1)}, bf16[512,128]{1,0:T(8,128)(2,1)}) custom-call(bf16[512,96]{1,0:T(8,128)(2,1)} %bitcast.8, s32[64,8]{1,0:T(8,128)} %bitcast.9, bf16[27,96,96]{2,1,0:T(8,128)(2,1)} %cw_ref.1, f32[1,128]{1,0:T(1,128)} %pad_bitcast_fusion.bias_ref, bf16[27,96,96]{2,1,0:T(8,128)(2,1)} %dw_ref.1, ...), custom_call_target="tpu_custom_call" | custom-call | tf_op jit(solution)/shard_map/pallas_call | solution.py:416
  66.2 0.0 copy-start
  66.2 1.2 %copy-done = bf16[2,2048,128]{2,1,0:T(8,128)(2,1)S(1)} copy-done((bf16[2,2048,128]{2,1,0:T(8,128)(2,1)S(1)}, bf16[2,2048,128]{2,1,0:T(8,128)(2,1)}, u32[]{:S(2)}) %copy-start) | copy-done | bytes 1048600
  67.5 0.0 copy-start.1
  67.5 0.9 %copy-done.1 = bf16[512,128]{1,0:T(8,128)(2,1)S(1)} copy-done((bf16[512,128]{1,0:T(8,128)(2,1)S(1)}, bf16[512,128]{1,0:T(8,128)(2,1)}, u32[]{:S(2)}) %copy-start.1) | copy-done | bytes 131096
  68.4 0.0 copy-start.2
  68.4 0.7 copy-done.2
  69.1 2.8 %shard_map.102 = (bf16[64,96]{1,0:T(8,128)(2,1)}, bf16[512,96]{1,0:T(8,128)(2,1)}, f32[27,96,96]{2,1,0:T(8,128)}, f32[1,96]{1,0:T(1,128)}, f32[27,96,96]{2,1,0:T(8,128)}) custom-call(bf16[2,2048,128]{2,1,0:T(8,128)(2,1)S(1)} %copy-done, bf16[64,128]{1,0:T(8,128)(2,1)S(1)} %copy-done.2, bf16[512,128]{1,0:T(8,128)(2,1)S(1)} %copy-done.1), custom_call_target="tpu_custom_call" | custom-call | tf_op jit(solution)/shard_map/pallas_call | solution.py:440
Async XLA Ops:
  66.2 1.2 %copy-start = (bf16[2,2048,128]{2,1,0:T(8,128)(2,1)S(1)}, bf16[2,2048,128]{2,1,0:T(8,128)(2,1)}, u32[]{:S(2)}) copy-start(bf16[2,2048,128]{2,1,0:T(8,128)(2,1)} %get-tuple-element.13.refs_0_) | copy-start | bytes 3145732
  67.5 0.9 %copy-start.1 = (bf16[512,128]{1,0:T(8,128)(2,1)S(1)}, bf16[512,128]{1,0:T(8,128)(2,1)}, u32[]{:S(2)}) copy-start(bf16[512,128]{1,0:T(8,128)(2,1)} %get-tuple-element.15.refs_2_) | copy-start | bytes 393220
  68.4 0.7 copy-start.2

commit v2 on v1

--- a/solution.py
+++ b/solution.py
@@ -90,12 +90,15 @@
 
 
 def main_kernel(
-    vox_ref, occ_ref, cw_ref, bias_ref, dw_ref, cot_ref,
+    vox_hbm, occ_hbm, cw_hbm, bias_hbm, dw_hbm, cot_hbm,
     fin_ref, down_ref, gv_ref,
+    vox_ref, occ_ref, cw_ref, bias_ref, dw_ref, cot_ref, bias_row,
     hs, hr, a3, c3, gs10, s3, g3, pre, p1, p2, ps, wf, wb, df, db, cl,
-    part, rc, xs, xr, ys, yr, zs, zr, zg,
-    h_send, h_recv, c_send, c_recv, x_send, x_recv, y_send, y_recv, z_send, z_recv,
-    zg_send, zg_recv, yg_send, yg_recv, xg_send, xg_recv, cg_send, cg_recv,
+    part, rc, xa, xa_in, nb, nb_in, na, na_in, xb, xb_in, far_in,
+    in_sem, h_send, h_recv, c_send, c_recv, xa_send, xa_recv, nb_send, nb_recv,
+    na_send, na_recv, xb_send, xb_recv, far_send, far_recv,
+    gna_send, gna_recv, gxb_send, gxb_recv, gnb_send, gnb_recv, gxa_send, gxa_recv,
+    gc_send, gc_recv,
 ):
     gx = lax.axis_index("gx")
     gy = lax.axis_index("gy")
@@ -122,11 +125,30 @@
     for peer in greeted:
         pl.semaphore_signal(barrier, inc=1, device_id=peer, device_id_type=MESH)
 
+    loads = [
+        pltpu.make_async_copy(src, dst, in_sem.at[i])
+        for i, (src, dst) in enumerate(
+            (
+                (occ_hbm, occ_ref),
+                (vox_hbm, vox_ref),
+                (cot_hbm, cot_ref),
+                (cw_hbm, cw_ref),
+                (dw_hbm, dw_ref),
+                (bias_hbm, bias_ref),
+            )
+        )
+    ]
+    for load in loads:
+        load.start()
+
     def remote(src, dst, send, recv, peer):
         return pltpu.make_async_remote_copy(
             src_ref=src, dst_ref=dst, send_sem=send, recv_sem=recv, device_id=peer,
             device_id_type=MESH,
         )
+
+    for load in loads[:3]:
+        load.wait()
 
     spread = (iota((512, 64), 0) // DEEP == iota((512, 64), 1)).astype(BF16)
     by_column = dot(spread, occ_ref[...].astype(F32).astype(BF16))
@@ -179,6 +201,10 @@
     store_shifts(c3, cot, 1, HALF, 1, HALF)
     for ref in (wf, wb, df, db):
         ref[...] = jnp.zeros(ref.shape, BF16)
+    bias_row[...] = jnp.zeros((1, LANES), F32)
+    for load in loads[3:]:
+        load.wait()
+    bias_row[:, 0:C] = bias_ref[...]
     for t in range(TAPS):
         for source, plain, turned in ((cw_ref, wf, wb), (dw_ref, df, db)):
             block = source[t]
@@ -212,7 +238,7 @@
             rows = wx * wy * DEEP
             window = a3[e + 1, x1 : x1 + wx, y1 : y1 + wy]
             p1[row : row + rows, lanes] = window.reshape(rows, LANES).astype(BF16)
-    pre[...] = dot(p1[...], wf[...]) + bias_ref[...]
+    pre[...] = dot(p1[...], wf[...]) + bias_row[...]
 
     for parity_x in (0, 1):
         for parity_y in (0, 1):
@@ -257,17 +283,26 @@
     for j, tile in enumerate(dense_tiles(acc, jnp.zeros((C, LANES), F32))):
         part[1, j * C : (j + 1) * C, :] = tile.astype(BF16)
 
-    order = (2, 1, 3, 0)
-    chunk = [pl.ds(pl.multiple_of(((px + k) % NX) * 512, 512), 512) for k in range(NX)]
-    core_copies = [
-        remote(part.at[1 - core, chunk[k]], rc.at[chunk[k]], c_send.at[k], c_recv.at[k], sibling)
-        for k in range(NX)
+    rows_a = [pl.ds(pl.multiple_of(((px + k) % NX) * 256, 256), 256) for k in range(NX)]
+    rows_b = [
+        pl.ds(pl.multiple_of(1024 + ((i_near + k) % 8) * 128, 128), 128) for k in range(8)
     ]
+    sibling_b = [
+        pl.ds(pl.multiple_of(1024 + ((i_far + k) % 8) * 128, 128), 128) for k in range(8)
+    ]
+    order = (("a", 2), ("b", 4), ("a", 1), ("b", 3), ("b", 5), ("a", 3))
+    order += (("b", 2), ("b", 6), ("a", 0), ("b", 1), ("b", 7), ("b", 0))
+    core_copies = []
+    for i, (which, k) in enumerate(order):
+        rows = rows_a[k] if which == "a" else sibling_b[k]
+        core_copies.append(
+            remote(part.at[1 - core, rows], rc.at[rows], c_send.at[i], c_recv.at[i], sibling)
+        )
 
     @pl.when(core == 0)
     def _():
-        for k in order:
-            core_copies[k].start()
+        for copy in core_copies:
+            copy.start()
 
     pre_turned = g3[1, 1:9, 1:9].reshape(512, LANES).T[0:C].astype(BF16)
     acc = dot(pre_turned, p1[0:512, :])
@@ -276,95 +311,147 @@
 
     @pl.when(core == 1)
     def _():
-        for k in order:
-            core_copies[k].start()
+        for copy in core_copies:
+            copy.start()
+
+    xa_copies, nb_copies = {}, {}
+    for copy, (which, k) in zip(core_copies, order):
+        copy.wait()
+        rows = rows_a[k] if which == "a" else rows_b[k]
+        both = (part[core, rows].astype(F32) + rc[rows].astype(F32)).astype(BF16)
+        if which == "a":
+            xa[k] = both
+            if k:
+                xa_copies[k] = remote(
+                    xa.at[k], xa_in.at[k], xa_send.at[k], xa_recv.at[k], x_peer[k]
+                )
+                xa_copies[k].start()
+        else:
+            nb[k] = both
+            if k:
+                nb_copies[k] = remote(
+                    nb.at[k], nb_in.at[k], nb_send.at[k], nb_recv.at[k], near[k]
+                )
+                nb_copies[k].start()
 
     downward = (iota((64, 128), 1) == 2 * iota((64, 128), 0)).astype(BF16)
     coarse = (dot(ps[...], df[...]) * cl[...]).astype(BF16)
-    down_ref[...] = dot(downward, coarse).astype(BF16)
-
-    x_copies = []
-    for k in order:
-        core_copies[k].wait()
-        both = part[core, chunk[k]].astype(F32) + rc[chunk[k]].astype(F32)
-        xs[k] = both.astype(BF16)
-        if k:
-            copy = remote(xs.at[k], xr.at[k], x_send.at[k], x_recv.at[k], x_peer[k])
-            copy.start()
-            x_copies.append(copy)
+    down_ref[...] = dot(downward, coarse).astype(BF16)[:, 0:C]
 
     for t, (a, b, e) in enumerate(TAP_OFFSETS):
         window = g3[1 - e, 1 - a : 9 - a, 1 - b : 9 - b]
         p2[:, t * LANES : (t + 1) * LANES] = window.reshape(512, LANES).astype(BF16)
     grad_in = ten[1:9, 1:9].reshape(512, LANES) + dot_nt(p2[...], wb[...])
     alive = dot(p1[0:512, 13 * LANES : 14 * LANES], pick_live)
-    gv_ref[...] = (grad_in * alive).astype(BF16)
-
-    for copy in x_copies:
-        copy.wait()
-    ys[...] = (
-        xs[0].astype(F32) + xr[1].astype(F32) + xr[2].astype(F32) + xr[3].astype(F32)
-    ).astype(BF16).reshape(8, 64, LANES)
+    gv_ref[...] = (grad_in * alive).astype(BF16)[:, 0:C]
+
+    far_first = (4, 3, 5, 2, 6, 1, 7)
+    total = xa[0].astype(F32)
+    for k in (1, 3, 2):
+        xa_copies[k].wait()
+        total = total + xa_in[k].astype(F32)
+    na[...] = total.reshape(8, 32, LANES).astype(BF16)
+    na_copies = {}
+    for k in far_first:
+        block = na.at[(i_near + k) % 8]
+        na_copies[k] = remote(block, na_in.at[k], na_send.at[k], na_recv.at[k], near[k])
+        na_copies[k].start()
+    total = nb[0].astype(F32)
+    for k in (1, 7, 2, 6, 3, 5, 4):
+        nb_copies[k].wait()
+        total = total + nb_in[k].astype(F32)
+    xb[...] = total.reshape(4, 32, LANES).astype(BF16)
+    xb_copies = {}
+    for k in (2, 1, 3):
+        block = xb.at[(px + k) % NX]
+        xb_copies[k] = remote(block, xb_in.at[k], xb_send.at[k], xb_recv.at[k], x_peer[k])
+        xb_copies[k].start()
+
+    total = xb[px].astype(F32)
+    for k in (1, 3, 2):
+        xb_copies[k].wait()
+        total = total + xb_in[k].astype(F32)
+    far_in[i_far, 32:64] = total.astype(BF16)
+    total = na[i_near].astype(F32)
+    for k in (1, 7, 2, 6, 3, 5, 4):
+        na_copies[k].wait()
+        total = total + na_in[k].astype(F32)
+    far_in[i_far, 0:32] = total.astype(BF16)
     copies = []
-    for k in (4, 3, 5, 2, 6, 1, 7):
-        block = ys.at[(i_near + k) % 8]
-        copies.append(remote(block, yr.at[k], y_send.at[k], y_recv.at[k], near[k]))
+    for k in far_first:
+        block = far_in.at[i_far]
+        copies.append(remote(block, block, far_send.at[k], far_recv.at[k], far[k]))
         copies[-1].start()
     for copy in copies:
         copy.wait()
-    total = ys[i_near].astype(F32)
+    total = far_in[0].astype(F32)
     for k in range(1, 8):
-        total = total + yr[k].astype(F32)
-    zs[...] = total.reshape(8, 8, LANES)
-    copies = []
-    for k in (4, 3, 5, 2, 6, 1, 7):
-        block = zs.at[(i_far + k) % 8]
-        copies.append(remote(block, zr.at[k], z_send.at[k], z_recv.at[k], far[k]))
-        copies[-1].start()
-    for copy in copies:
-        copy.wait()
-    total = zs[i_far]
-    for k in range(1, 8):
-        total = total + zr[k]
-
-    zg[i_far] = total
-    copies = []
-    for k in (4, 3, 5, 2, 6, 1, 7):
-        block = zg.at[i_far]
-        copies.append(remote(block, block, zg_send.at[k], zg_recv.at[k], far[k]))
-        copies[-1].start()
-    for copy in copies:
-        copy.wait()
-    own = pl.ds(pl.multiple_of(px * 512 + i_near * 64, 64), 64)
-    fin_ref[core, own] = zg[...].reshape(64, LANES).astype(BF16)
-    copies = []
-    for k in (4, 3, 5, 2, 6, 1, 7):
-        block = fin_ref.at[core, own]
-        copies.append(remote(block, block, yg_send.at[k], yg_recv.at[k], near[k]))
-        copies[-1].start()
-    for copy in copies:
-        copy.wait()
-    copies = {}
+        total = total + far_in[k].astype(F32)
+    total = total.astype(BF16)
+
+    own_a = pl.ds(pl.multiple_of(px * 256 + i_near * 32, 32), 32)
+    own_b = pl.ds(pl.multiple_of(1024 + i_near * 128 + px * 32, 32), 32)
+    fin_ref[core, own_a] = total[0:32]
+    fin_ref[core, own_b] = total[32:64]
+    gxb_copies, gna_copies, gnb_copies, gxa_copies = {}, {}, {}, {}
     for k in (2, 1, 3):
-        block = fin_ref.at[core, chunk[0]]
-        copies[k] = remote(block, block, xg_send.at[k], xg_recv.at[k], x_peer[k])
-        copies[k].start()
+        block = fin_ref.at[core, own_b]
+        gxb_copies[k] = remote(block, block, gxb_send.at[k], gxb_recv.at[k], x_peer[k])
+        gxb_copies[k].start()
+    for k in far_first:
+        block = fin_ref.at[core, own_a]
+        gna_copies[k] = remote(block, block, gna_send.at[k], gna_recv.at[k], near[k])
+        gna_copies[k].start()
+    for k in (1, 3, 2):
+        gxb_copies[k].wait()
+    for k in far_first:
+        block = fin_ref.at[core, rows_b[0]]
+        gnb_copies[k] = remote(block, block, gnb_send.at[k], gnb_recv.at[k], near[k])
+        gnb_copies[k].start()
+    for k in (1, 7, 2, 6, 3, 5, 4):
+        gna_copies[k].wait()
+    for k in (2, 1, 3):
+        block = fin_ref.at[core, rows_a[0]]
+        gxa_copies[k] = remote(block, block, gxa_send.at[k], gxa_recv.at[k], x_peer[k])
+        gxa_copies[k].start()
     last = []
-    for k in (0, 1, 3, 2):
-        if k:
-            copies[k].wait()
-        block = fin_ref.at[core, chunk[-k % NX]]
-        last.append(remote(block, block, cg_send.at[k], cg_recv.at[k], sibling))
+
+    def hand_over(rows):
+        i = len(last)
+        block = fin_ref.at[core, rows]
+        last.append(remote(block, block, gc_send.at[i], gc_recv.at[i], sibling))
         last[-1].start()
+
+    hand_over(rows_b[0])
+    hand_over(rows_a[0])
+    for which, k in (
+        ("b", 1), ("b", 7), ("a", 1), ("a", 3), ("b", 2), ("b", 6), ("b", 3), ("b", 5), ("a", 2),
+        ("b", 4),
+    ):
+        if which == "a":
+            gxa_copies[k].wait()
+            hand_over(rows_a[-k % NX])
+        else:
+            gnb_copies[k].wait()
+            hand_over(rows_b[-k % 8])
     for copy in last:
         copy.wait()
 
 
-def finish_kernel(factor, fin_ref, down_in, gv_in, down_ref, gv_ref, gc_ref, gb_ref, gd_ref):
-    down_ref[...] = down_in[:, 0:C]
-    gv_ref[...] = gv_in[:, 0:C]
+def finish_kernel(
+    factor, fin_ref, down_in, gv_in, down_ref, gv_ref, gc_ref, gb_ref, gd_ref,
+    gc, gb, gd, sem,
+):
+    copies = []
+
+    def send_out(src, dst):
+        copies.append(pltpu.make_async_copy(src, dst, sem.at[len(copies)]))
+        copies[-1].start()
+
+    send_out(down_in, down_ref)
+    send_out(gv_in, gv_ref)
     lane = iota((C, LANES), 1)
-    for w, out in ((0, gc_ref), (1, gd_ref)):
+    for w, held, out in ((1, gd, gd_ref), (0, gc, gc_ref)):
         for group in range(7):
             first, second, third = (
                 fin_ref[w, (3 * group + i) * C : (3 * group + i + 1) * C, :].astype(F32) * factor
@@ -376,16 +463,29 @@
                 pltpu.roll(jnp.where(lane >= 64, second, third), 64, 1),
                 pltpu.roll(third, 96, 1),
             ]
-            for i in range(4 if group < 6 else 3):
-                out[4 * group + i] = taps[i].T[0:C]
+            count = 4 if group < 6 else 3
+            for i in range(count):
+                held[4 * group + i] = taps[i].T[0:C]
+            block = pl.ds(4 * group, count)
+            send_out(held.at[block], out.at[block])
         if w == 0:
-            gb_ref[...] = third.T[32:33]
+            gb[...] = third.T[32:33]
+            send_out(gb, gb_ref)
+    for copy in copies:
+        copy.wait()
 
 
 def on_device(voxels, occupancy, conv_weight, conv_bias, down_weight, down_cotangent):
     vmem = pl.BlockSpec(memory_space=pltpu.VMEM)
-    bias = jnp.pad(conv_bias, (0, LANES - C)).reshape(1, LANES)
+    anywhere = pl.BlockSpec(memory_space=pl.ANY)
     scratch = [
+        ((512, C), BF16),
+        ((64, DEEP), jnp.int32),
+        ((TAPS, C, C), BF16),
+        ((1, C), F32),
+        ((TAPS, C, C), BF16),
+        ((64, C), BF16),
+        ((1, LANES), F32),
         ((HALO_ROWS, LANES), BF16),
         ((HALO_ROWS, LANES), BF16),
         ((3, 12, 12, DEEP, LANES), F32),
@@ -404,23 +504,25 @@
         ((128, LANES), F32),
         ((2, ROWS, LANES), BF16),
         ((ROWS, LANES), BF16),
-        ((4, 512, LANES), BF16),
-        ((4, 512, LANES), BF16),
+        ((4, 256, LANES), BF16),
+        ((4, 256, LANES), BF16),
+        ((8, 128, LANES), BF16),
+        ((8, 128, LANES), BF16),
+        ((8, 32, LANES), BF16),
+        ((8, 32, LANES), BF16),
+        ((4, 32, LANES), BF16),
+        ((4, 32, LANES), BF16),
         ((8, 64, LANES), BF16),
-        ((8, 64, LANES), BF16),
-        ((8, 8, LANES), F32),
-        ((8, 8, LANES), F32),
-        ((8, 8, LANES), F32),
     ]
-    semaphores = [8, 8, 4, 4, 4, 4, 8, 8, 8, 8, 8, 8, 8, 8, 4, 4, 4, 4]
+    semaphores = [6, 8, 8, 12, 12, 4, 4, 8, 8, 8, 8, 4, 4, 8, 8, 8, 8, 4, 4, 8, 8, 4, 4, 12, 12]
     fin, down, grad_voxels = pl.pallas_call(
         main_kernel,
         out_shape=(
-            jax.ShapeDtypeStruct((2, ROWS, LANES), BF16),
-            jax.ShapeDtypeStruct((64, LANES), BF16),
-            jax.ShapeDtypeStruct((512, LANES), BF16),
+            pltpu.VMEM((2, ROWS, LANES), BF16),
+            pltpu.VMEM((64, C), BF16),
+            pltpu.VMEM((512, C), BF16),
         ),
-        in_specs=[vmem] * 6,
+        in_specs=[anywhere] * 6,
         out_specs=(vmem, vmem, vmem),
         scratch_shapes=[pltpu.VMEM(shape, dtype) for shape, dtype in scratch]
         + [pltpu.SemaphoreType.DMA((n,)) for n in semaphores],
@@ -431,7 +533,7 @@
         voxels.reshape(512, C),
         occupancy.reshape(64, DEEP),
         conv_weight,
-        bias,
+        conv_bias.reshape(1, C),
         down_weight,
         down_cotangent.reshape(64, C),
     )
@@ -447,7 +549,13 @@
             jax.ShapeDtypeStruct((TAPS, C, C), F32),
         ),
         in_specs=[vmem] * 3,
-        out_specs=(vmem,) * 5,
+        out_specs=(anywhere,) * 5,
+        scratch_shapes=[
+            pltpu.VMEM((TAPS, C, C), F32),
+            pltpu.VMEM((1, C), F32),
+            pltpu.VMEM((TAPS, C, C), F32),
+            pltpu.SemaphoreType.DMA((17,)),
+        ],
         compiler_params=pltpu.CompilerParams(vmem_limit_bytes=32 * 1024 * 1024),
     )(fin, down, grad_voxels)
     return (

time: 72.1 us -> 57.6 us (0.80)
  Pallas kernels: 67.2 us -> 56.8 us
  local copies, waits for them, and re-layouts: 4.01 us -> 0 us
    pallas_call x1, Pallas kernels: 64.4 us -> 54.5 us  [on_device(): pl.pallas_call(main_kernel, out_shape=(pltpu.VMEM((2, ROWS, LANES), BF16)...]
    unnamed x6 -> x0, local copies, waits for them, and re-layouts: 2.84 us -> none
    reshape x1 -> x0, local copies, waits for them, and re-layouts: 1.17 us -> none  [on_device(): bias = jnp.pad(conv_bias, (0, LANES - C)).reshape(1, LANES)]
where the time goes in v2:
time: 57.6 us; the launch traced here: 57.5 us
  Pallas kernels  56.8 us (99%)
  between operations  0.64 us (1%)
    pallas_call x1, Pallas kernels, on_device(): pl.pallas_call(main_kernel, out_shape=(pltpu.VMEM((2, ROWS, LANES), BF16)...  54.5 us
    pallas_call x1, Pallas kernels, on_device(): pl.pallas_call(lambda *refs: finish_kernel(factor, *refs), out_shape=(jax...  2.29 us

profile of v2, /device:TPU:1, one launch (start us, length us, event | category | flops | bytes accessed | tf_op | source)
XLA Modules:
  0.0 57.5 jit_solution(9859030353036211122)
XLA Ops:
  0.6 54.5 %shard_map.101 = (bf16[2,2048,128]{2,1,0:T(8,128)(2,1)S(1)}, bf16[64,96]{1,0:T(8,128)(2,1)S(1)}, bf16[512,96]{1,0:T(8,128)(2,1)S(1)}) custom-call(bf16[512,96]{1,0:T(8,128)(2,1)} %bitcast.7, s32[64,8]{1,0:T(8,128)} %bitcast.8, bf16[27,96,96]{2,1,0:T(8,128)(2,1)} %cw_hbm.1, f32[1,96]{1,0:T(1,128)} %bitcast.10, bf16[27,96,96]{2,1,0:T(8,128)(2,1)} %dw_hbm.1, ...), custom_call_target="tpu_custom_call" | custom-call | tf_op jit(solution)/shard_map/pallas_call | solution.py:518
  55.2 2.3 %shard_map.102 = (bf16[64,96]{1,0:T(8,128)(2,1)}, bf16[512,96]{1,0:T(8,128)(2,1)}, f32[27,96,96]{2,1,0:T(8,128)}, f32[1,96]{1,0:T(1,128)}, f32[27,96,96]{2,1,0:T(8,128)}) custom-call(bf16[2,2048,128]{2,1,0:T(8,128)(2,1)S(1)} %get-tuple-element.13.refs_0_, bf16[64,96]{1,0:T(8,128)(2,1)S(1)} %get-tuple-element.14.refs_1_, ...), custom_call_target="tpu_custom_call" | custom-call | tf_op jit(solution)/shard_map/pallas_call | solution.py:542

commit v3 on v2

--- a/solution.py
+++ b/solution.py
@@ -19,6 +19,7 @@
 DEEP = 8
 K_ALL = TAPS * LANES
 ROWS = 2048
+PARTS = ((0, 32), (1024, 32))
 NX, NY, NZ = 4, 8, 8
 TAP_OFFSETS = [(a, b, e) for a in (-1, 0, 1) for b in (-1, 0, 1) for e in (-1, 0, 1)]
 
@@ -147,6 +148,9 @@
             device_id_type=MESH,
         )
 
+    def await_bytes(ref, semaphore):
+        pltpu.make_async_copy(ref, ref, semaphore).wait()
+
     for load in loads[:3]:
         load.wait()
 
@@ -188,14 +192,12 @@
         hs[at + rows : at + SIDE_ROWS[i], :] = block.astype(BF16)
 
     pl.semaphore_wait(barrier, len(greeted))
-    halo = []
     for i, (sx, sy) in enumerate(SIDES):
         there = SIDES.index((-sx, -sy))
         mine = pl.ds(SIDE_AT[i], SIDE_ROWS[i])
         theirs = pl.ds(SIDE_AT[there], SIDE_ROWS[i])
-        copy = remote(hs.at[mine], hr.at[theirs], h_send.at[i], h_recv.at[there], side_peer[i])
+        copy = remote(hs.at[mine], hr.at[theirs], h_send.at[0], h_recv.at[0], side_peer[i])
         copy.start()
-        halo.append(copy)
 
     store_shifts(a3, masked, 2, TILE, 2, TILE)
     store_shifts(c3, cot, 1, HALF, 1, HALF)
@@ -213,8 +215,8 @@
     for w in (0, 1):
         part[w, 2016:2048, :] = jnp.zeros((32, LANES), BF16)
 
-    for copy in halo:
-        copy.wait()
+    await_bytes(hs, h_send.at[0])
+    await_bytes(hr, h_recv.at[0])
     for i, (sx, sy) in enumerate(SIDES):
         inside = 1.0
         for step, at, size in ((sx, gx, n_gx), (sy, gy, n_gy)):
@@ -278,61 +280,66 @@
         j0, sj = (b + 1) // 2, (b + 1) % 2
         window = six[e + 1, i0 : i0 + 4, si, j0 : j0 + 4, sj]
         ps[:, t * LANES : (t + 1) * LANES] = window.reshape(128, LANES).astype(BF16)
-    cot_turned = c3[1, 1:5, 1:5].reshape(128, LANES).T[0:C].astype(BF16)
-    acc = dot(cot_turned, ps[...])
-    for j, tile in enumerate(dense_tiles(acc, jnp.zeros((C, LANES), F32))):
-        part[1, j * C : (j + 1) * C, :] = tile.astype(BF16)
-
-    rows_a = [pl.ds(pl.multiple_of(((px + k) % NX) * 256, 256), 256) for k in range(NX)]
-    rows_b = [
-        pl.ds(pl.multiple_of(1024 + ((i_near + k) % 8) * 128, 128), 128) for k in range(8)
-    ]
-    sibling_b = [
-        pl.ds(pl.multiple_of(1024 + ((i_far + k) % 8) * 128, 128), 128) for k in range(8)
-    ]
-    order = (("a", 2), ("b", 4), ("a", 1), ("b", 3), ("b", 5), ("a", 3))
-    order += (("b", 2), ("b", 6), ("a", 0), ("b", 1), ("b", 7), ("b", 0))
+    far_first = (4, 3, 5, 2, 6, 1, 7)
+    near_first = (1, 7, 2, 6, 3, 5, 4)
+
+    def rows(which, place):
+        start, size = PARTS[which]
+        return pl.ds(pl.multiple_of(start + place * 4 * size, 64), 4 * size)
+
+    def block_rows(which, place, x):
+        start, size = PARTS[which]
+        return pl.ds(pl.multiple_of(start + place * 4 * size + x * size, 16), size)
+
+    order = [(which, j) for j in far_first + (0,) for which in (0, 1)]
     core_copies = []
-    for i, (which, k) in enumerate(order):
-        rows = rows_a[k] if which == "a" else sibling_b[k]
+    for which, j in order:
+        there = rows(which, (i_far + j) % 8)
         core_copies.append(
-            remote(part.at[1 - core, rows], rc.at[rows], c_send.at[i], c_recv.at[i], sibling)
+            remote(part.at[1 - core, there], rc.at[there], c_send.at[0], c_recv.at[j], sibling)
         )
+
+    def down_sums():
+        cot_turned = c3[1, 1:5, 1:5].reshape(128, LANES).T[0:C].astype(BF16)
+        acc = dot(cot_turned, ps[...])
+        for j, tile in enumerate(dense_tiles(acc, jnp.zeros((C, LANES), F32))):
+            part[1, j * C : (j + 1) * C, :] = tile.astype(BF16)
+
+    def conv_sums():
+        pre_turned = g3[1, 1:9, 1:9].reshape(512, LANES).T[0:C].astype(BF16)
+        acc = dot(pre_turned, p1[0:512, :])
+        for j, tile in enumerate(dense_tiles(acc, acc[:, 13 * LANES : 14 * LANES])):
+            part[0, j * C : (j + 1) * C, :] = tile.astype(BF16)
 
     @pl.when(core == 0)
     def _():
+        down_sums()
         for copy in core_copies:
             copy.start()
-
-    pre_turned = g3[1, 1:9, 1:9].reshape(512, LANES).T[0:C].astype(BF16)
-    acc = dot(pre_turned, p1[0:512, :])
-    for j, tile in enumerate(dense_tiles(acc, acc[:, 13 * LANES : 14 * LANES])):
-        part[0, j * C : (j + 1) * C, :] = tile.astype(BF16)
+        conv_sums()
 
     @pl.when(core == 1)
     def _():
+        conv_sums()
         for copy in core_copies:
             copy.start()
-
-    xa_copies, nb_copies = {}, {}
-    for copy, (which, k) in zip(core_copies, order):
-        copy.wait()
-        rows = rows_a[k] if which == "a" else rows_b[k]
-        both = (part[core, rows].astype(F32) + rc[rows].astype(F32)).astype(BF16)
-        if which == "a":
-            xa[k] = both
-            if k:
-                xa_copies[k] = remote(
-                    xa.at[k], xa_in.at[k], xa_send.at[k], xa_recv.at[k], x_peer[k]
-                )
-                xa_copies[k].start()
+        down_sums()
+
+    for which, j in order:
+        if which == 0:
+            await_bytes(rc.at[0:256], c_recv.at[j])
+        here = rows(which, (i_near + j) % 8)
+        both = (part[core, here].astype(F32) + rc[here].astype(F32)).astype(BF16)
+        if which == 0:
+            xa[j] = both.reshape(4, 32, LANES)
+            for k in (2, 1, 3):
+                remote(
+                    xa.at[j, (px + k) % NX], xa_in.at[j, k], xa_send.at[0], xa_recv.at[j], x_peer[k]
+                ).start()
         else:
-            nb[k] = both
-            if k:
-                nb_copies[k] = remote(
-                    nb.at[k], nb_in.at[k], nb_send.at[k], nb_recv.at[k], near[k]
-                )
-                nb_copies[k].start()
+            nb[j] = both
+            if j:
+                remote(nb.at[j], nb_in.at[j], nb_send.at[0], nb_recv.at[0], near[j]).start()
 
     downward = (iota((64, 128), 1) == 2 * iota((64, 128), 0)).astype(BF16)
     coarse = (dot(ps[...], df[...]) * cl[...]).astype(BF16)
@@ -345,97 +352,91 @@
     alive = dot(p1[0:512, 13 * LANES : 14 * LANES], pick_live)
     gv_ref[...] = (grad_in * alive).astype(BF16)[:, 0:C]
 
-    far_first = (4, 3, 5, 2, 6, 1, 7)
-    total = xa[0].astype(F32)
-    for k in (1, 3, 2):
-        xa_copies[k].wait()
-        total = total + xa_in[k].astype(F32)
-    na[...] = total.reshape(8, 32, LANES).astype(BF16)
-    na_copies = {}
-    for k in far_first:
-        block = na.at[(i_near + k) % 8]
-        na_copies[k] = remote(block, na_in.at[k], na_send.at[k], na_recv.at[k], near[k])
-        na_copies[k].start()
+    for j in far_first + (0,):
+        await_bytes(xa_in.at[j, 1:4], xa_recv.at[j])
+        total = xa[j, px].astype(F32)
+        for k in (1, 3, 2):
+            total = total + xa_in[j, k].astype(F32)
+        na[j] = total.astype(BF16)
+        if j:
+            remote(na.at[j], na_in.at[j], na_send.at[0], na_recv.at[0], near[j]).start()
+    await_bytes(nb_in.at[1:8], nb_recv.at[0])
     total = nb[0].astype(F32)
-    for k in (1, 7, 2, 6, 3, 5, 4):
-        nb_copies[k].wait()
+    for k in near_first:
         total = total + nb_in[k].astype(F32)
     xb[...] = total.reshape(4, 32, LANES).astype(BF16)
-    xb_copies = {}
     for k in (2, 1, 3):
-        block = xb.at[(px + k) % NX]
-        xb_copies[k] = remote(block, xb_in.at[k], xb_send.at[k], xb_recv.at[k], x_peer[k])
-        xb_copies[k].start()
-
+        remote(xb.at[(px + k) % NX], xb_in.at[k], xb_send.at[0], xb_recv.at[0], x_peer[k]).start()
+
+    await_bytes(na_in.at[1:8], na_recv.at[0])
+    total = na[0].astype(F32)
+    for k in near_first:
+        total = total + na_in[k].astype(F32)
+    far_in[i_far, 0:32] = total.astype(BF16)
+    await_bytes(xb_in.at[1:4], xb_recv.at[0])
     total = xb[px].astype(F32)
     for k in (1, 3, 2):
-        xb_copies[k].wait()
         total = total + xb_in[k].astype(F32)
     far_in[i_far, 32:64] = total.astype(BF16)
-    total = na[i_near].astype(F32)
-    for k in (1, 7, 2, 6, 3, 5, 4):
-        na_copies[k].wait()
-        total = total + na_in[k].astype(F32)
-    far_in[i_far, 0:32] = total.astype(BF16)
-    copies = []
     for k in far_first:
         block = far_in.at[i_far]
-        copies.append(remote(block, block, far_send.at[k], far_recv.at[k], far[k]))
-        copies[-1].start()
-    for copy in copies:
-        copy.wait()
+        remote(block, block, far_send.at[0], far_recv.at[0], far[k]).start()
+    await_bytes(far_in.at[0:7], far_recv.at[0])
     total = far_in[0].astype(F32)
     for k in range(1, 8):
         total = total + far_in[k].astype(F32)
     total = total.astype(BF16)
 
-    own_a = pl.ds(pl.multiple_of(px * 256 + i_near * 32, 32), 32)
-    own_b = pl.ds(pl.multiple_of(1024 + i_near * 128 + px * 32, 32), 32)
-    fin_ref[core, own_a] = total[0:32]
-    fin_ref[core, own_b] = total[32:64]
-    gxb_copies, gna_copies, gnb_copies, gxa_copies = {}, {}, {}, {}
+    fin_ref[core, block_rows(0, i_near, px)] = total[0:32]
+    fin_ref[core, block_rows(1, i_near, px)] = total[32:64]
+
+    block = fin_ref.at[core, block_rows(0, i_near, px)]
+    for k in far_first:
+        remote(block, block, gna_send.at[0], gna_recv.at[k], near[k]).start()
+    block = fin_ref.at[core, block_rows(1, i_near, px)]
     for k in (2, 1, 3):
-        block = fin_ref.at[core, own_b]
-        gxb_copies[k] = remote(block, block, gxb_send.at[k], gxb_recv.at[k], x_peer[k])
-        gxb_copies[k].start()
+        remote(block, block, gxb_send.at[0], gxb_recv.at[0], x_peer[k]).start()
+
+    def across(j):
+        if j:
+            await_bytes(na_in.at[j], gna_recv.at[j])
+        block = fin_ref.at[core, block_rows(0, (i_near - j + 8) % 8, px)]
+        for k in (2, 1, 3):
+            remote(block, block, gxa_send.at[0], gxa_recv.at[j], x_peer[k]).start()
+
+    def hand_over(which, j):
+        block = fin_ref.at[core, rows(which, (i_near - j + 8) % 8)]
+        remote(block, block, gc_send.at[0], gc_recv.at[0], sibling).start()
+
+    for j in (0, 1, 7):
+        across(j)
+    await_bytes(xb_in.at[1:4], gxb_recv.at[0])
+    block = fin_ref.at[core, rows(1, i_near)]
     for k in far_first:
-        block = fin_ref.at[core, own_a]
-        gna_copies[k] = remote(block, block, gna_send.at[k], gna_recv.at[k], near[k])
-        gna_copies[k].start()
-    for k in (1, 3, 2):
-        gxb_copies[k].wait()
-    for k in far_first:
-        block = fin_ref.at[core, rows_b[0]]
-        gnb_copies[k] = remote(block, block, gnb_send.at[k], gnb_recv.at[k], near[k])
-        gnb_copies[k].start()
-    for k in (1, 7, 2, 6, 3, 5, 4):
-        gna_copies[k].wait()
-    for k in (2, 1, 3):
-        block = fin_ref.at[core, rows_a[0]]
-        gxa_copies[k] = remote(block, block, gxa_send.at[k], gxa_recv.at[k], x_peer[k])
-        gxa_copies[k].start()
-    last = []
-
-    def hand_over(rows):
-        i = len(last)
-        block = fin_ref.at[core, rows]
-        last.append(remote(block, block, gc_send.at[i], gc_recv.at[i], sibling))
-        last[-1].start()
-
-    hand_over(rows_b[0])
-    hand_over(rows_a[0])
-    for which, k in (
-        ("b", 1), ("b", 7), ("a", 1), ("a", 3), ("b", 2), ("b", 6), ("b", 3), ("b", 5), ("a", 2),
-        ("b", 4),
+        remote(block, block, gnb_send.at[0], gnb_recv.at[k], near[k]).start()
+    for j in (2, 6, 3, 5, 4):
+        across(j)
+    for j in (0,) + near_first:
+        await_bytes(xa_in.at[j, 1:4], gxa_recv.at[j])
+        hand_over(0, j)
+        if j:
+            await_bytes(nb_in.at[j], gnb_recv.at[j])
+        hand_over(1, j)
+    for ref, sends in (
+        (rc, c_send),
+        (xa_in.at[:, 1:4], xa_send),
+        (nb_in.at[1:8], nb_send),
+        (na_in.at[1:8], na_send),
+        (xb_in.at[1:4], xb_send),
+        (far_in.at[0:7], far_send),
+        (na_in.at[1:8], gna_send),
+        (xb_in.at[1:4], gxb_send),
+        (xa_in.at[:, 1:4], gxa_send),
+        (nb_in.at[1:8], gnb_send),
+        (rc, gc_send),
+        (rc, gc_recv),
     ):
-        if which == "a":
-            gxa_copies[k].wait()
-            hand_over(rows_a[-k % NX])
-        else:
-            gnb_copies[k].wait()
-            hand_over(rows_b[-k % 8])
-    for copy in last:
-        copy.wait()
+        await_bytes(ref, sends.at[0])
 
 
 def finish_kernel(
@@ -504,8 +505,8 @@
         ((128, LANES), F32),
         ((2, ROWS, LANES), BF16),
         ((ROWS, LANES), BF16),
-        ((4, 256, LANES), BF16),
-        ((4, 256, LANES), BF16),
+        ((8, 4, 32, LANES), BF16),
+        ((8, 4, 32, LANES), BF16),
         ((8, 128, LANES), BF16),
         ((8, 128, LANES), BF16),
         ((8, 32, LANES), BF16),
@@ -514,7 +515,7 @@
         ((4, 32, LANES), BF16),
         ((8, 64, LANES), BF16),
     ]
-    semaphores = [6, 8, 8, 12, 12, 4, 4, 8, 8, 8, 8, 4, 4, 8, 8, 8, 8, 4, 4, 8, 8, 4, 4, 12, 12]
+    semaphores = [6, 1, 1, 1, 8, 1, 8, 1, 1, 1, 1, 1, 1, 1, 1, 1, 8, 1, 1, 1, 8, 1, 8, 1, 1]
     fin, down, grad_voxels = pl.pallas_call(
         main_kernel,
         out_shape=(

time: 57.6 us -> 53.8 us (0.934)
  Pallas kernels: 56.8 us -> 53 us
    pallas_call x1, Pallas kernels: 54.5 us -> 50.7 us  [on_device(): pl.pallas_call(main_kernel, out_shape=(pltpu.VMEM((2, ROWS, LANES), BF16)...]
where the time goes in v3:
time: 53.8 us; the launch traced here: 53.6 us
  Pallas kernels  53 us (99%)
  between operations  0.64 us (1%)
    pallas_call x1, Pallas kernels, on_device(): pl.pallas_call(main_kernel, out_shape=(pltpu.VMEM((2, ROWS, LANES), BF16)...  50.7 us
    pallas_call x1, Pallas kernels, on_device(): pl.pallas_call(lambda *refs: finish_kernel(factor, *refs), out_shape=(jax...  2.29 us

profile of v3, /device:TPU:1, one launch (start us, length us, event | category | flops | bytes accessed | tf_op | source)
XLA Modules:
  0.0 53.6 jit_solution(17092812343528513964)
XLA Ops:
  0.6 50.7 %shard_map.101 = (bf16[2,2048,128]{2,1,0:T(8,128)(2,1)S(1)}, bf16[64,96]{1,0:T(8,128)(2,1)S(1)}, bf16[512,96]{1,0:T(8,128)(2,1)S(1)}) custom-call(bf16[512,96]{1,0:T(8,128)(2,1)} %bitcast.7, s32[64,8]{1,0:T(8,128)} %bitcast.8, bf16[27,96,96]{2,1,0:T(8,128)(2,1)} %cw_hbm.1, f32[1,96]{1,0:T(1,128)} %bitcast.10, bf16[27,96,96]{2,1,0:T(8,128)(2,1)} %dw_hbm.1, ...), custom_call_target="tpu_custom_call" | custom-call | tf_op jit(solution)/shard_map/pallas_call | solution.py:519
  51.4 2.3 %shard_map.102 = (bf16[64,96]{1,0:T(8,128)(2,1)}, bf16[512,96]{1,0:T(8,128)(2,1)}, f32[27,96,96]{2,1,0:T(8,128)}, f32[1,96]{1,0:T(1,128)}, f32[27,96,96]{2,1,0:T(8,128)}) custom-call(bf16[2,2048,128]{2,1,0:T(8,128)(2,1)S(1)} %get-tuple-element.13.refs_0_, bf16[64,96]{1,0:T(8,128)(2,1)S(1)} %get-tuple-element.14.refs_1_, ...), custom_call_target="tpu_custom_call" | custom-call | tf_op jit(solution)/shard_map/pallas_call | solution.py:543

commit v4 on v3

--- a/solution.py
+++ b/solution.py
@@ -122,7 +122,9 @@
     i_far = pz + core * (py - pz)
 
     barrier = pltpu.get_barrier_semaphore()
-    greeted = side_peer + [sibling] + x_peer[1:] + y_peer[1:] + z_peer[1:]
+    greeted = [peer for k in (4, 3, 5, 2, 6) for peer in (y_peer[k], z_peer[k])]
+    greeted += [x_peer[2]] + side_peer[4:] + [x_peer[1], x_peer[3]]
+    greeted += [y_peer[1], z_peer[1], y_peer[7], z_peer[7]] + side_peer[:4]
     for peer in greeted:
         pl.semaphore_signal(barrier, inc=1, device_id=peer, device_id_type=MESH)
 
@@ -192,7 +194,8 @@
         hs[at + rows : at + SIDE_ROWS[i], :] = block.astype(BF16)
 
     pl.semaphore_wait(barrier, len(greeted))
-    for i, (sx, sy) in enumerate(SIDES):
+    for i in (4, 5, 6, 7, 0, 1, 2, 3):
+        sx, sy = SIDES[i]
         there = SIDES.index((-sx, -sy))
         mine = pl.ds(SIDE_AT[i], SIDE_ROWS[i])
         theirs = pl.ds(SIDE_AT[there], SIDE_ROWS[i])
@@ -341,17 +344,6 @@
             if j:
                 remote(nb.at[j], nb_in.at[j], nb_send.at[0], nb_recv.at[0], near[j]).start()
 
-    downward = (iota((64, 128), 1) == 2 * iota((64, 128), 0)).astype(BF16)
-    coarse = (dot(ps[...], df[...]) * cl[...]).astype(BF16)
-    down_ref[...] = dot(downward, coarse).astype(BF16)[:, 0:C]
-
-    for t, (a, b, e) in enumerate(TAP_OFFSETS):
-        window = g3[1 - e, 1 - a : 9 - a, 1 - b : 9 - b]
-        p2[:, t * LANES : (t + 1) * LANES] = window.reshape(512, LANES).astype(BF16)
-    grad_in = ten[1:9, 1:9].reshape(512, LANES) + dot_nt(p2[...], wb[...])
-    alive = dot(p1[0:512, 13 * LANES : 14 * LANES], pick_live)
-    gv_ref[...] = (grad_in * alive).astype(BF16)[:, 0:C]
-
     for j in far_first + (0,):
         await_bytes(xa_in.at[j, 1:4], xa_recv.at[j])
         total = xa[j, px].astype(F32)
@@ -381,6 +373,18 @@
     for k in far_first:
         block = far_in.at[i_far]
         remote(block, block, far_send.at[0], far_recv.at[0], far[k]).start()
+
+    downward = (iota((64, 128), 1) == 2 * iota((64, 128), 0)).astype(BF16)
+    coarse = (dot(ps[...], df[...]) * cl[...]).astype(BF16)
+    down_ref[...] = dot(downward, coarse).astype(BF16)[:, 0:C]
+
+    for t, (a, b, e) in enumerate(TAP_OFFSETS):
+        window = g3[1 - e, 1 - a : 9 - a, 1 - b : 9 - b]
+        p2[:, t * LANES : (t + 1) * LANES] = window.reshape(512, LANES).astype(BF16)
+    grad_in = ten[1:9, 1:9].reshape(512, LANES) + dot_nt(p2[...], wb[...])
+    alive = dot(p1[0:512, 13 * LANES : 14 * LANES], pick_live)
+    gv_ref[...] = (grad_in * alive).astype(BF16)[:, 0:C]
+
     await_bytes(far_in.at[0:7], far_recv.at[0])
     total = far_in[0].astype(F32)
     for k in range(1, 8):
@@ -405,6 +409,10 @@
             remote(block, block, gxa_send.at[0], gxa_recv.at[j], x_peer[k]).start()
 
     def hand_over(which, j):
+        if which == 0:
+            await_bytes(xa_in.at[j, 1:4], gxa_recv.at[j])
+        elif j:
+            await_bytes(nb_in.at[j], gnb_recv.at[j])
         block = fin_ref.at[core, rows(which, (i_near - j + 8) % 8)]
         remote(block, block, gc_send.at[0], gc_recv.at[0], sibling).start()
 
@@ -414,14 +422,17 @@
     block = fin_ref.at[core, rows(1, i_near)]
     for k in far_first:
         remote(block, block, gnb_send.at[0], gnb_recv.at[k], near[k]).start()
-    for j in (2, 6, 3, 5, 4):
+    hand_over(1, 0)
+    for j in (2, 6):
         across(j)
-    for j in (0,) + near_first:
-        await_bytes(xa_in.at[j, 1:4], gxa_recv.at[j])
-        hand_over(0, j)
-        if j:
-            await_bytes(nb_in.at[j], gnb_recv.at[j])
-        hand_over(1, j)
+    hand_over(0, 0)
+    for j in (3, 5, 4):
+        across(j)
+    for which, j in (
+        (0, 1), (0, 7), (1, 1), (1, 7), (0, 2), (0, 6), (1, 2), (1, 6), (0, 3), (0, 5), (0, 4),
+        (1, 3), (1, 5), (1, 4),
+    ):
+        hand_over(which, j)
     for ref, sends in (
         (rc, c_send),
         (xa_in.at[:, 1:4], xa_send),
@@ -451,26 +462,17 @@
 
     send_out(down_in, down_ref)
     send_out(gv_in, gv_ref)
-    lane = iota((C, LANES), 1)
+    unit = (iota((LANES, LANES), 0) == iota((LANES, LANES), 1)).astype(BF16)
     for w, held, out in ((1, gd, gd_ref), (0, gc, gc_ref)):
-        for group in range(7):
-            first, second, third = (
-                fin_ref[w, (3 * group + i) * C : (3 * group + i + 1) * C, :].astype(F32) * factor
-                for i in range(3)
-            )
-            taps = [
-                first,
-                pltpu.roll(jnp.where(lane >= 96, first, second), 32, 1),
-                pltpu.roll(jnp.where(lane >= 64, second, third), 64, 1),
-                pltpu.roll(third, 96, 1),
-            ]
-            count = 4 if group < 6 else 3
-            for i in range(count):
-                held[4 * group + i] = taps[i].T[0:C]
-            block = pl.ds(4 * group, count)
-            send_out(held.at[block], out.at[block])
+        for j in range(21):
+            turned = dot_nt(unit, fin_ref[w, j * C : (j + 1) * C, :]) * factor
+            count = min(LANES, TAPS * C - j * LANES)
+            held[j * LANES : j * LANES + count, :] = turned[0:count]
+            if j % 3 == 2:
+                block = pl.ds((j - 2) * LANES, 2 * LANES + count)
+                send_out(held.at[block], out.at[block])
         if w == 0:
-            gb[...] = third.T[32:33]
+            gb[...] = turned[32:33]
             send_out(gb, gb_ref)
     for copy in copies:
         copy.wait()
@@ -545,16 +547,16 @@
         out_shape=(
             jax.ShapeDtypeStruct((64, C), BF16),
             jax.ShapeDtypeStruct((512, C), BF16),
-            jax.ShapeDtypeStruct((TAPS, C, C), F32),
+            jax.ShapeDtypeStruct((TAPS * C, C), F32),
             jax.ShapeDtypeStruct((1, C), F32),
-            jax.ShapeDtypeStruct((TAPS, C, C), F32),
+            jax.ShapeDtypeStruct((TAPS * C, C), F32),
         ),
         in_specs=[vmem] * 3,
         out_specs=(anywhere,) * 5,
         scratch_shapes=[
-            pltpu.VMEM((TAPS, C, C), F32),
+            pltpu.VMEM((TAPS * C, C), F32),
             pltpu.VMEM((1, C), F32),
-            pltpu.VMEM((TAPS, C, C), F32),
+            pltpu.VMEM((TAPS * C, C), F32),
             pltpu.SemaphoreType.DMA((17,)),
         ],
         compiler_params=pltpu.CompilerParams(vmem_limit_bytes=32 * 1024 * 1024),
@@ -562,9 +564,9 @@
     return (
         down.reshape(down_cotangent.shape),
         grad_voxels.reshape(voxels.shape),
-        grad_conv,
+        grad_conv.reshape(TAPS, C, C),
         grad_bias.reshape(C),
-        grad_down,
+        grad_down.reshape(TAPS, C, C),
     )
 
 

time: 53.8 us -> 52.9 us (0.983)
  Pallas kernels: 53 us -> 52.1 us
where the time goes in v4:
time: 52.9 us; the launch traced here: 52.7 us
  Pallas kernels  52.1 us (98%)
  between operations  0.64 us (1%)
    pallas_call x1, Pallas kernels, on_device(): pl.pallas_call(main_kernel, out_shape=(pltpu.VMEM((2, ROWS, LANES), BF16)...  50.2 us
    pallas_call x1, Pallas kernels, on_device(): pl.pallas_call(lambda *refs: finish_kernel(factor, *refs), out_shape=(jax...  1.87 us

profile of v4, /device:TPU:1, one launch (start us, length us, event | category | flops | bytes accessed | tf_op | source)
XLA Modules:
  0.0 52.7 jit_solution(15860277281242785677)
XLA Ops:
  0.6 50.2 %shard_map.101 = (bf16[2,2048,128]{2,1,0:T(8,128)(2,1)S(1)}, bf16[64,96]{1,0:T(8,128)(2,1)S(1)}, bf16[512,96]{1,0:T(8,128)(2,1)S(1)}) custom-call(bf16[512,96]{1,0:T(8,128)(2,1)} %bitcast.9, s32[64,8]{1,0:T(8,128)} %bitcast.10, bf16[27,96,96]{2,1,0:T(8,128)(2,1)} %cw_hbm.1, f32[1,96]{1,0:T(1,128)} %bitcast.12, bf16[27,96,96]{2,1,0:T(8,128)(2,1)} %dw_hbm.1, ...), custom_call_target="tpu_custom_call" | custom-call | tf_op jit(solution)/shard_map/pallas_call | solution.py:521
  50.9 1.9 %shard_map.102 = (bf16[64,96]{1,0:T(8,128)(2,1)}, bf16[512,96]{1,0:T(8,128)(2,1)}, f32[2592,96]{1,0:T(8,128)}, f32[1,96]{1,0:T(1,128)}, f32[2592,96]{1,0:T(8,128)}) custom-call(bf16[2,2048,128]{2,1,0:T(8,128)(2,1)S(1)} %get-tuple-element.13.refs_0_, bf16[64,96]{1,0:T(8,128)(2,1)S(1)} %get-tuple-element.14.refs_1_, bf16[512,96]{1,0:T(8,128)(2,1)S(1)} %get-tuple-element.15.refs_2_), custom_call_target="tpu_custom_call" | custom-call | tf_op jit(solution)/shard_map/pallas_call | solution.py:545

commit v5 on v4

--- a/solution.py
+++ b/solution.py
@@ -294,7 +294,7 @@
         start, size = PARTS[which]
         return pl.ds(pl.multiple_of(start + place * 4 * size + x * size, 16), size)
 
-    order = [(which, j) for j in far_first + (0,) for which in (0, 1)]
+    order = [(which, j) for j in far_first + (0,) for which in (1, 0)]
     core_copies = []
     for which, j in order:
         there = rows(which, (i_far + j) % 8)
@@ -329,7 +329,7 @@
         down_sums()
 
     for which, j in order:
-        if which == 0:
+        if which == 1:
             await_bytes(rc.at[0:256], c_recv.at[j])
         here = rows(which, (i_near + j) % 8)
         both = (part[core, here].astype(F32) + rc[here].astype(F32)).astype(BF16)
@@ -394,12 +394,12 @@
     fin_ref[core, block_rows(0, i_near, px)] = total[0:32]
     fin_ref[core, block_rows(1, i_near, px)] = total[32:64]
 
+    block = fin_ref.at[core, block_rows(1, i_near, px)]
+    for k in (2, 1, 3):
+        remote(block, block, gxb_send.at[0], gxb_recv.at[0], x_peer[k]).start()
     block = fin_ref.at[core, block_rows(0, i_near, px)]
     for k in far_first:
         remote(block, block, gna_send.at[0], gna_recv.at[k], near[k]).start()
-    block = fin_ref.at[core, block_rows(1, i_near, px)]
-    for k in (2, 1, 3):
-        remote(block, block, gxb_send.at[0], gxb_recv.at[0], x_peer[k]).start()
 
     def across(j):
         if j:

time: 52.9 us -> 52.9 us (level)
  no operation moved by 1% of the time
where the time goes in v5:
time: 52.9 us; the launch traced here: 52.7 us
  Pallas kernels  52.1 us (98%)
  between operations  0.64 us (1%)
    pallas_call x1, Pallas kernels, on_device(): pl.pallas_call(main_kernel, out_shape=(pltpu.VMEM((2, ROWS, LANES), BF16)...  50.2 us
    pallas_call x1, Pallas kernels, on_device(): pl.pallas_call(lambda *refs: finish_kernel(factor, *refs), out_shape=(jax...  1.87 us

profile of v5, /device:TPU:1, one launch (start us, length us, event | category | flops | bytes accessed | tf_op | source)
XLA Modules:
  0.0 52.7 jit_solution(2573881676775763304)
XLA Ops:
  0.6 50.2 %shard_map.101 = (bf16[2,2048,128]{2,1,0:T(8,128)(2,1)S(1)}, bf16[64,96]{1,0:T(8,128)(2,1)S(1)}, bf16[512,96]{1,0:T(8,128)(2,1)S(1)}) custom-call(bf16[512,96]{1,0:T(8,128)(2,1)} %bitcast.9, s32[64,8]{1,0:T(8,128)} %bitcast.10, bf16[27,96,96]{2,1,0:T(8,128)(2,1)} %cw_hbm.1, f32[1,96]{1,0:T(1,128)} %bitcast.12, bf16[27,96,96]{2,1,0:T(8,128)(2,1)} %dw_hbm.1, ...), custom_call_target="tpu_custom_call" | custom-call | tf_op jit(solution)/shard_map/pallas_call | solution.py:521
  50.8 1.9 %shard_map.102 = (bf16[64,96]{1,0:T(8,128)(2,1)}, bf16[512,96]{1,0:T(8,128)(2,1)}, f32[2592,96]{1,0:T(8,128)}, f32[1,96]{1,0:T(1,128)}, f32[2592,96]{1,0:T(8,128)}) custom-call(bf16[2,2048,128]{2,1,0:T(8,128)(2,1)S(1)} %get-tuple-element.13.refs_0_, bf16[64,96]{1,0:T(8,128)(2,1)S(1)} %get-tuple-element.14.refs_1_, bf16[512,96]{1,0:T(8,128)(2,1)S(1)} %get-tuple-element.15.refs_2_), custom_call_target="tpu_custom_call" | custom-call | tf_op jit(solution)/shard_map/pallas_call | solution.py:545
